TPU v7x, 256 devices: a whole 4x4x8 slice. The times are simulated.
256 devices in a mesh: dp: 32 (over x, z), seq: 8 (over y, core).
Axes of the slice: x: 4, y: 4, z: 8, core: 2. Of those that a mesh axis runs over, the one named last changes fastest.
Arguments:
- query: bfloat16 [32768, 4096], P(('dp', 'seq')), may hold values from -64 to 64
- key_states: bfloat16 [32768, 1024], P(('dp', 'seq')), may hold values from -16 to 16
- value_states: bfloat16 [32768, 1024], P(('dp', 'seq')), may hold values from -6 to 6
- out_grad: bfloat16 [32768, 4096], P(('dp', 'seq')), may hold values from -6 to 6
- target_group: int32 [32768], P(('dp', 'seq')), may hold values from 0 to 31, as said below
- document: int32 [32768], P(('dp', 'seq')), may hold values from 0 to 1
Outputs:
- attention_out: bfloat16 [32768, 4096], P(('dp', 'seq'))
- query_grad: bfloat16 [32768, 4096], P(('dp', 'seq'))
- key_grad: bfloat16 [32768, 1024], P(('dp', 'seq'))
- value_grad: bfloat16 [32768, 1024], P(('dp', 'seq'))
Inputs may be any that keep to these rules, and one draw needn't show every extreme that they name: `target_group`: the 128 rows of one device name each group at most 5 times. In every draw, for each index of seq, some group is named exactly 5 times by the rows of every device with that index of seq.
All inputs are finite; a program needn't handle non-finite values.
Results may differ from a plain program's by a relative error of at most 0.035.
Values may be sent and summed in bfloat16 or wider, within the bound.
A program may use at most 128 MiB of HBM per device.

v0:
```python
import math

import jax
import jax.numpy as jnp
from jax import lax
from jax.sharding import PartitionSpec as P

HD = 128


def attend_one(q_head, k_head, v_head, g_head, allowed, row_valid):
    inv_root = 1.0 / math.sqrt(q_head.shape[1])
    scores = jnp.einsum("qd,kd->qk", q_head, k_head, preferred_element_type=jnp.float32) * inv_root
    scores = jnp.where(allowed, scores, -1e30)
    row_max = jnp.max(scores, axis=1, keepdims=True)
    exp_scores = jnp.where(allowed, jnp.exp(scores - row_max), 0.0)
    row_total = jnp.where(row_valid[:, None], jnp.sum(exp_scores, axis=1, keepdims=True), 1.0)
    probs_full = exp_scores / row_total
    probs_low = probs_full.astype(jnp.bfloat16)
    attn_out = jnp.einsum(
        "qk,kd->qd", probs_low, v_head, preferred_element_type=jnp.float32
    ).astype(jnp.bfloat16)
    delta_row = jnp.sum(
        g_head.astype(jnp.float32) * attn_out.astype(jnp.float32), axis=1, keepdims=True
    )
    prob_grad = jnp.einsum("qd,kd->qk", g_head, v_head, preferred_element_type=jnp.float32)
    score_grad = (probs_full * (prob_grad - delta_row)).astype(jnp.bfloat16)
    q_grad = (
        jnp.einsum("qk,kd->qd", score_grad, k_head, preferred_element_type=jnp.float32) * inv_root
    ).astype(jnp.bfloat16)
    k_grad = (
        jnp.einsum("qk,qd->kd", score_grad, q_head, preferred_element_type=jnp.float32) * inv_root
    )
    v_grad = jnp.einsum("qk,qd->kd", probs_low, g_head, preferred_element_type=jnp.float32)
    return (attn_out, q_grad, k_grad, v_grad)


def attend_heads(q_rows, k_rows, v_rows, g_rows, meta_query, meta_key):
    head_size = HD
    q_count = q_rows.shape[1] // head_size
    kv_count = k_rows.shape[1] // head_size
    head_ratio = q_count // kv_count
    query_rows = q_rows.shape[0]
    key_rows = k_rows.shape[0]
    doc_query = meta_query[:, 1]
    doc_key = meta_key[:, 1]
    row_valid = doc_query >= 0
    allowed = (
        (doc_query[:, None] == doc_key[None, :])
        & row_valid[:, None]
        & (meta_key[None, :, 0] <= meta_query[:, None, 0])
    )

    def per_kv(kv_index):
        k_head = lax.dynamic_slice_in_dim(k_rows, kv_index * head_size, head_size, 1)
        v_head = lax.dynamic_slice_in_dim(v_rows, kv_index * head_size, head_size, 1)

        def per_query_head(running, inner_index):
            head_index = kv_index * head_ratio + inner_index
            q_head = lax.dynamic_slice_in_dim(q_rows, head_index * head_size, head_size, 1)
            g_head = lax.dynamic_slice_in_dim(g_rows, head_index * head_size, head_size, 1)
            attn_out, q_grad, k_grad, v_grad = attend_one(
                q_head, k_head, v_head, g_head, allowed, row_valid
            )
            return ((running[0] + k_grad, running[1] + v_grad), (attn_out, q_grad))

        zero_grad = jnp.zeros((key_rows, head_size), jnp.float32)
        grad_sums, head_outs = lax.scan(
            per_query_head, (zero_grad, zero_grad), jnp.arange(head_ratio, dtype=jnp.int32)
        )
        return (head_outs[0], head_outs[1], grad_sums[0], grad_sums[1])

    attn_out, q_grad, k_grad, v_grad = lax.map(per_kv, jnp.arange(kv_count, dtype=jnp.int32))
    attn_out = (
        attn_out.reshape(q_count, query_rows, head_size)
        .transpose(1, 0, 2)
        .reshape(query_rows, q_count * head_size)
    )
    q_grad = (
        q_grad.reshape(q_count, query_rows, head_size)
        .transpose(1, 0, 2)
        .reshape(query_rows, q_count * head_size)
    )
    k_grad = k_grad.transpose(1, 0, 2).reshape(key_rows, kv_count * head_size)
    v_grad = v_grad.transpose(1, 0, 2).reshape(key_rows, kv_count * head_size)
    return (attn_out, q_grad, k_grad, v_grad)


def per_device(query, key_states, value_states, out_grad, target_group, document):
    tok_rows = query.shape[0]
    dp_count = lax.axis_size("dp")
    seq_count = lax.axis_size("seq")
    capacity = max(2, (5 * tok_rows + 4 * dp_count - 1) // (4 * dp_count))
    slot_count = dp_count * capacity
    row_line = jnp.arange(tok_rows, dtype=jnp.int32)
    same_group = target_group[:, None] == target_group[None, :]
    earlier = row_line[None, :] < row_line[:, None]
    rank_in_group = jnp.sum((same_group & earlier).astype(jnp.int32), axis=1)
    slot = target_group * capacity + rank_in_group
    first_row = (lax.axis_index("dp") * seq_count + lax.axis_index("seq")) * tok_rows
    position = first_row + row_line

    def pack_rows(rows):
        return jnp.zeros((slot_count, rows.shape[1]), rows.dtype).at[slot].set(rows)

    packed = (pack_rows(query), pack_rows(key_states), pack_rows(value_states), pack_rows(out_grad))
    blank = jnp.concatenate(
        [jnp.zeros((slot_count, 1), jnp.int32), -jnp.ones((slot_count, 1), jnp.int32)], axis=1
    )
    ident_rows = blank.at[slot].set(jnp.stack([position, document], axis=1))
    meta_group = lax.all_to_all(
        lax.all_to_all(
            jnp.tile(ident_rows, (1, seq_count)), "dp", split_axis=0, concat_axis=0, tiled=True
        ),
        "seq",
        split_axis=1,
        concat_axis=0,
        tiled=True,
    )
    q_local, k_local, v_local, g_local = (
        lax.all_to_all(packed[0], "dp", split_axis=0, concat_axis=0, tiled=True),
        lax.all_to_all(packed[1], "dp", split_axis=0, concat_axis=0, tiled=True),
        lax.all_to_all(packed[2], "dp", split_axis=0, concat_axis=0, tiled=True),
        lax.all_to_all(packed[3], "dp", split_axis=0, concat_axis=0, tiled=True),
    )
    k_all, v_all = (
        lax.all_gather(k_local, "seq", axis=0, tiled=True),
        lax.all_gather(v_local, "seq", axis=0, tiled=True),
    )
    meta_mine = lax.dynamic_slice_in_dim(
        meta_group, lax.axis_index("seq") * slot_count, slot_count, 0
    )
    attn_out, q_grad, k_terms, v_terms = attend_heads(
        q_local, k_all, v_all, g_local, meta_mine, meta_group
    )
    k_grad, v_grad = (
        lax.psum_scatter(k_terms, "seq", scatter_dimension=0, tiled=True),
        lax.psum_scatter(v_terms, "seq", scatter_dimension=0, tiled=True),
    )
    returned = (
        lax.all_to_all(attn_out, "dp", split_axis=0, concat_axis=0, tiled=True),
        lax.all_to_all(q_grad, "dp", split_axis=0, concat_axis=0, tiled=True),
        lax.all_to_all(k_grad.astype(jnp.bfloat16), "dp", split_axis=0, concat_axis=0, tiled=True),
        lax.all_to_all(v_grad.astype(jnp.bfloat16), "dp", split_axis=0, concat_axis=0, tiled=True),
    )
    return tuple((piece[slot] for piece in returned))


def solution(mesh):
    return jax.shard_map(
        per_device,
        mesh=mesh,
        in_specs=(
            P(("dp", "seq"), None),
            P(("dp", "seq"), None),
            P(("dp", "seq"), None),
            P(("dp", "seq"), None),
            P(("dp", "seq")),
            P(("dp", "seq")),
        ),
        out_specs=(
            P(("dp", "seq"), None),
            P(("dp", "seq"), None),
            P(("dp", "seq"), None),
            P(("dp", "seq"), None),
        ),
        check_vma=False,
    )
```

profile of v0, /device:TPU:32, one launch (start us, length us, event | category | flops | bytes accessed | tf_op | source)
XLA Modules:
  0.0 704.9 jit_solution(3187188547796293785)
XLA Ops:
  10.6 28.7 %all_to_all.124 = bf16[32,5,1024]{2,1,0:T(8,128)(2,1)S(1)} all-to-all(bf16[32,5,1024]{2,1,0:T(8,128)(2,1)S(1)} %all_to_all.84), channel_id=1, replica_groups=mesh['dp'=32,'seq'=8] {'dp'}, dimensions={0} | all-to-all | bytes 655360 | tf_op jit(solution)/shard_map/all_to_all | solution.py:122
  42.0 14.4 %all_to_all.125 = s32[32,5,16]{2,1,0:T(8,128)S(1)} all-to-all(s32[32,5,16]{2,1,0:T(8,128)S(1)} %copy.45), channel_id=1, replica_groups=mesh['dp'=32,'seq'=8] {'dp'}, dimensions={0} | all-to-all | bytes 20480 | tf_op jit(solution)/shard_map/all_to_all | solution.py:112
  76.5 13.3 %all-to-all-done.1 = bf16[32,5,1024]{2,1,0:T(8,128)(2,1)S(1)} async-done(((bf16[32,5,1024]{2,1,0:T(8,128)(2,1)}), bf16[32,5,1024]{2,1,0:T(8,128)(2,1)S(1)}, u32[]{:S(2)}, u32[]{:S(2)}) %all-to-all-start.1) | async-done | bytes 327712 | tf_op jit(solution)/shard_map/all_to_all | solution.py:123
  100.3 43.2 %all-to-all-done.5 = bf16[32,5,4096]{2,1,0:T(8,128)(2,1)S(1)} async-done(((bf16[32,5,4096]{2,1,0:T(8,128)(2,1)}), bf16[32,5,4096]{2,1,0:T(8,128)(2,1)S(1)}, u32[]{:S(2)}, u32[]{:S(2)}) %all-to-all-start.5) | async-done | bytes 1310752 | tf_op jit(solution)/shard_map/all_to_all | solution.py:124
  143.5 7.1 %all-to-all-start.2 = ((bf16[32,5,4096]{2,1,0:T(8,128)(2,1)}), bf16[32,5,4096]{2,1,0:T(8,128)(2,1)}, u32[]{:S(2)}, u32[]{:S(2)}) async-start(bf16[32,5,4096]{2,1,0:T(8,128)(2,1)} %all_to_all.90), calls=%async_computation.2 | async-start | bytes 4194304 | tf_op jit(solution)/shard_map/all_to_all | solution.py:121
  152.7 47.4 %all-to-all-done.2 = bf16[32,5,4096]{2,1,0:T(8,128)(2,1)} async-done(((bf16[32,5,4096]{2,1,0:T(8,128)(2,1)}), bf16[32,5,4096]{2,1,0:T(8,128)(2,1)}, u32[]{:S(2)}, u32[]{:S(2)}) %all-to-all-start.2) | async-done | bytes 1310752 | tf_op jit(solution)/shard_map/all_to_all | solution.py:121
  202.7 319.7 %while.38 = (s32[]{:T(128)}, bf16[8,4,160,128]{3,2,1,0:T(8,128)(2,1)}, bf16[8,4,160,128]{3,2,1,0:T(8,128)(2,1)}, f32[8,1280,128]{1,2,0:T(8,128)}, f32[8,1280,128...) while((s32[]{:T(128)}, ...), condition=%wide.region_12.13_spmd.clone, body=%wide.region_6.12_spmd.clone.sunk | while | flops 320450240 | bytes 18085268 | solution.py:73
  207.0 33.2 %while.39 = (s32[]{:T(128)}, f32[1280,128]{1,0:T(8,128)S(1)}, f32[1280,128]{1,0:T(8,128)S(1)}, bf16[4,160,128]{2,1,0:T(8,128)(2,1)S(1)}, bf16[4,160,128]{2,1,0:T...) while((s32[]{:T(128)}, f32[1280,128]{1,0:T(8,128)S(1)}, ...), condition=%wide.region_11.11_spmd.clone, body=%wide.region_7.10_spmd.clone.sunk | while | flops 319631040 | bytes 10658346 | solution.py:68
  247.0 33.2 %while.39 = (s32[]{:T(128)}, f32[1280,128]{1,0:T(8,128)S(1)}, f32[1280,128]{1,0:T(8,128)S(1)}, bf16[4,160,128]{2,1,0:T(8,128)(2,1)S(1)}, bf16[4,160,128]{2,1,0:T...) while((s32[]{:T(128)}, f32[1280,128]{1,0:T(8,128)S(1)}, ...), condition=%wide.region_11.11_spmd.clone, body=%wide.region_7.10_spmd.clone.sunk | while | flops 319631040 | bytes 10658346 | solution.py:68
  286.9 33.2 %while.39 = (s32[]{:T(128)}, f32[1280,128]{1,0:T(8,128)S(1)}, f32[1280,128]{1,0:T(8,128)S(1)}, bf16[4,160,128]{2,1,0:T(8,128)(2,1)S(1)}, bf16[4,160,128]{2,1,0:T...) while((s32[]{:T(128)}, f32[1280,128]{1,0:T(8,128)S(1)}, ...), condition=%wide.region_11.11_spmd.clone, body=%wide.region_7.10_spmd.clone.sunk | while | flops 319631040 | bytes 10658346 | solution.py:68
  326.9 33.2 %while.39 = (s32[]{:T(128)}, f32[1280,128]{1,0:T(8,128)S(1)}, f32[1280,128]{1,0:T(8,128)S(1)}, bf16[4,160,128]{2,1,0:T(8,128)(2,1)S(1)}, bf16[4,160,128]{2,1,0:T...) while((s32[]{:T(128)}, f32[1280,128]{1,0:T(8,128)S(1)}, ...), condition=%wide.region_11.11_spmd.clone, body=%wide.region_7.10_spmd.clone.sunk | while | flops 319631040 | bytes 10658346 | solution.py:68
  366.8 33.2 %while.39 = (s32[]{:T(128)}, f32[1280,128]{1,0:T(8,128)S(1)}, f32[1280,128]{1,0:T(8,128)S(1)}, bf16[4,160,128]{2,1,0:T(8,128)(2,1)S(1)}, bf16[4,160,128]{2,1,0:T...) while((s32[]{:T(128)}, f32[1280,128]{1,0:T(8,128)S(1)}, ...), condition=%wide.region_11.11_spmd.clone, body=%wide.region_7.10_spmd.clone.sunk | while | flops 319631040 | bytes 10658346 | solution.py:68
  406.8 33.2 %while.39 = (s32[]{:T(128)}, f32[1280,128]{1,0:T(8,128)S(1)}, f32[1280,128]{1,0:T(8,128)S(1)}, bf16[4,160,128]{2,1,0:T(8,128)(2,1)S(1)}, bf16[4,160,128]{2,1,0:T...) while((s32[]{:T(128)}, f32[1280,128]{1,0:T(8,128)S(1)}, ...), condition=%wide.region_11.11_spmd.clone, body=%wide.region_7.10_spmd.clone.sunk | while | flops 319631040 | bytes 10658346 | solution.py:68
  446.9 33.2 %while.39 = (s32[]{:T(128)}, f32[1280,128]{1,0:T(8,128)S(1)}, f32[1280,128]{1,0:T(8,128)S(1)}, bf16[4,160,128]{2,1,0:T(8,128)(2,1)S(1)}, bf16[4,160,128]{2,1,0:T...) while((s32[]{:T(128)}, f32[1280,128]{1,0:T(8,128)S(1)}, ...), condition=%wide.region_11.11_spmd.clone, body=%wide.region_7.10_spmd.clone.sunk | while | flops 319631040 | bytes 10658346 | solution.py:68
  486.8 33.2 %while.39 = (s32[]{:T(128)}, f32[1280,128]{1,0:T(8,128)S(1)}, f32[1280,128]{1,0:T(8,128)S(1)}, bf16[4,160,128]{2,1,0:T(8,128)(2,1)S(1)}, bf16[4,160,128]{2,1,0:T...) while((s32[]{:T(128)}, f32[1280,128]{1,0:T(8,128)S(1)}, ...), condition=%wide.region_11.11_spmd.clone, body=%wide.region_7.10_spmd.clone.sunk | while | flops 319631040 | bytes 10658346 | solution.py:68
  522.4 5.9 copy.54
  528.4 5.9 copy.56
  538.6 6.4 all-to-all-start.7
  549.4 45.1 %all-to-all-done.7 = bf16[32,5,4096]{2,1,0:T(8,128)(2,1)S(1)} async-done(((bf16[32,5,4096]{2,1,0:T(8,128)(2,1)}), bf16[32,5,4096]{2,1,0:T(8,128)(2,1)S(1)}, u32[]{:S(2)}, u32[]{:S(2)}) %all-to-all-start.7) | async-done | bytes 1310752 | tf_op jit(solution)/shard_map/all_to_all | solution.py:142
  594.5 6.4 all-to-all-start.6
  603.0 47.3 %all-to-all-done.6 = bf16[32,5,4096]{2,1,0:T(8,128)(2,1)} async-done(((bf16[32,5,4096]{2,1,0:T(8,128)(2,1)}), bf16[32,5,4096]{2,1,0:T(8,128)(2,1)}, u32[]{:S(2)}, u32[]{:S(2)}) %all-to-all-start.6) | async-done | bytes 1310752 | tf_op jit(solution)/shard_map/all_to_all | solution.py:141
  650.3 6.3 all-to-all-start.8
  658.7 15.0 %all-to-all-done.8 = bf16[32,5,1024]{2,1,0:T(8,128)(2,1)S(1)} async-done(((bf16[32,5,1024]{2,1,0:T(8,128)(2,1)}), bf16[32,5,1024]{2,1,0:T(8,128)(2,1)S(1)}, u32[]{:S(2)}, u32[]{:S(2)}) %all-to-all-start.8) | async-done | bytes 327712 | tf_op jit(solution)/shard_map/all_to_all | solution.py:143
  687.2 8.4 %all-to-all-done.9 = bf16[32,5,1024]{2,1,0:T(8,128)(2,1)} async-done(((bf16[32,5,1024]{2,1,0:T(8,128)(2,1)}), bf16[32,5,1024]{2,1,0:T(8,128)(2,1)}, u32[]{:S(2)}, u32[]{:S(2)}) %all-to-all-start.9) | async-done | bytes 327712 | tf_op jit(solution)/shard_map/all_to_all | solution.py:144
  (507 shorter events, 356.6 us)
Async XLA Ops:
  7.2 195.5 %all-gather.3.cloned.1.call-start = ((), (), s32[]{:S(2)}) async-start(), calls=%async_computation.12 | async-start | bytes 2949120 | tf_op jit(solution)/shard_map/all_gather | solution.py:127
  8.8 86.8 %copy-start.4 = (s32[128]{0:T(128)}, s32[128]{0:T(128)S(1)}, u32[]{:S(2)}) copy-start(s32[128]{0:T(128)S(1)} %compare_select_fusion) | copy-start | bytes 1540
  10.6 29.7 %copy-start.6 = (s32[128]{0:T(128)S(1)}, s32[128]{0:T(128)}, u32[]{:S(2)}) copy-start(s32[128]{0:T(128)} %param.15) | copy-start | bytes 1540
  10.6 29.8 %copy-start = (s32[160,2]{1,0:T(8,128)S(1)}, s32[160,2]{1,0:T(8,128)}, u32[]{:S(2)}) copy-start(s32[160,2]{1,0:T(8,128)} %constant.97.clone.1) | copy-start | bytes 3844
  57.5 9.8 %all-to-all-start.4 = ((s32[160,8,2]{0,2,1:T(2,128)}), s32[160,8,2]{0,2,1:T(2,128)S(1)}, u32[]{:S(2)}, u32[]{:S(2)}) async-start(s32[160,8,2]{0,2,1:T(2,128)} %all_to_all.95), calls=%async_computation.4 | async-start | bytes 32768 | tf_op jit(solution)/shard_map/all_to_all | solution.py:111
  67.3 22.4 %all-to-all-start.1 = ((bf16[32,5,1024]{2,1,0:T(8,128)(2,1)}), bf16[32,5,1024]{2,1,0:T(8,128)(2,1)S(1)}, u32[]{:S(2)}, u32[]{:S(2)}) async-start(bf16[32,5,1024]{2,1,0:T(8,128)(2,1)} %all_to_all.87), calls=%async_computation.1 | async-start | bytes 1048576 | tf_op jit(solution)/shard_map/all_to_all | solution.py:123
  89.8 53.8 %all-to-all-start.5 = ((bf16[32,5,4096]{2,1,0:T(8,128)(2,1)}), bf16[32,5,4096]{2,1,0:T(8,128)(2,1)S(1)}, u32[]{:S(2)}, u32[]{:S(2)}) async-start(bf16[32,5,4096]{2,1,0:T(8,128)(2,1)} %all_to_all.99), calls=%async_computation.5 | async-start | bytes 4194304 | tf_op jit(solution)/shard_map/all_to_all | solution.py:124
  94.7 108.1 %all-gather.5.cloned.1.call-start = ((), (), s32[]{:S(2)}) async-start(), calls=%async_computation.13 | async-start | bytes 2949120 | tf_op jit(solution)/shard_map/all_gather | solution.py:128
  143.5 56.5 %all-to-all-start.2 = ((bf16[32,5,4096]{2,1,0:T(8,128)(2,1)}), bf16[32,5,4096]{2,1,0:T(8,128)(2,1)}, u32[]{:S(2)}, u32[]{:S(2)}) async-start(bf16[32,5,4096]{2,1,0:T(8,128)(2,1)} %all_to_all.90), calls=%async_computation.2 | async-start | bytes 4194304 | tf_op jit(solution)/shard_map/all_to_all | solution.py:121
  150.6 450.2 %reduce-scatter.7.cloned.1.call-start = ((), (), s32[]{:S(2)}) async-start(), calls=%async_computation.14 | async-start | bytes 5898240 | tf_op jit(solution)/shard_map/reduce_scatter | solution.py:137
  528.4 128.3 %reduce-scatter.9.cloned.1.call-start = ((), (), s32[]{:S(2)}) async-start(), calls=%async_computation.15 | async-start | bytes 5898240 | tf_op jit(solution)/shard_map/reduce_scatter | solution.py:138
  534.4 1.3 copy-start.3
  538.6 55.9 %all-to-all-start.7 = ((bf16[32,5,4096]{2,1,0:T(8,128)(2,1)}), bf16[32,5,4096]{2,1,0:T(8,128)(2,1)S(1)}, u32[]{:S(2)}, u32[]{:S(2)}) async-start(bf16[32,5,4096]{2,1,0:T(8,128)(2,1)} %all_to_all.105), calls=%async_computation.7 | async-start | bytes 4194304 | tf_op jit(solution)/shard_map/all_to_all | solution.py:142
  594.5 55.8 %all-to-all-start.6 = ((bf16[32,5,4096]{2,1,0:T(8,128)(2,1)}), bf16[32,5,4096]{2,1,0:T(8,128)(2,1)}, u32[]{:S(2)}, u32[]{:S(2)}) async-start(bf16[32,5,4096]{2,1,0:T(8,128)(2,1)} %all_to_all.102), calls=%async_computation.6 | async-start | bytes 4194304 | tf_op jit(solution)/shard_map/all_to_all | solution.py:141
  650.3 23.5 %all-to-all-start.8 = ((bf16[32,5,1024]{2,1,0:T(8,128)(2,1)}), bf16[32,5,1024]{2,1,0:T(8,128)(2,1)S(1)}, u32[]{:S(2)}, u32[]{:S(2)}) async-start(bf16[32,5,1024]{2,1,0:T(8,128)(2,1)} %all_to_all.108), calls=%async_computation.8 | async-start | bytes 1048576 | tf_op jit(solution)/shard_map/all_to_all | solution.py:143
  656.6 22.1 %copy-start.5 = (s32[128]{0:T(128)S(1)}, s32[128]{0:T(128)}, u32[]{:S(2)}) copy-start(s32[128]{0:T(128)} %copy-done.4) | copy-start | bytes 1540
  673.8 4.9 copy-start.1
  673.8 21.8 %all-to-all-start.9 = ((bf16[32,5,1024]{2,1,0:T(8,128)(2,1)}), bf16[32,5,1024]{2,1,0:T(8,128)(2,1)}, u32[]{:S(2)}, u32[]{:S(2)}) async-start(bf16[32,5,1024]{2,1,0:T(8,128)(2,1)} %all_to_all.111), calls=%async_computation.9 | async-start | bytes 1048576 | tf_op jit(solution)/shard_map/all_to_all | solution.py:144
  683.3 2.2 copy-start.2
Sparse Core Ops, SparseCore 0:
  40.3 24.9 all-gather.2
  97.9 27.8 all-gather.4
  528.5 38.6 reduce-scatter.6
  569.7 42.6 reduce-scatter.8
where the time goes:
time: 717 us; the launch traced here: 705 us
  waiting for transfers between devices  223 us (31%)
  matrix products  212 us (30%)
  local copies, waits for them, and re-layouts  117 us (16%)
  starting transfers between devices  45.3 us (6%)
  blocking collectives  43.1 us (6%)
  loops' own time  33.3 us (5%)
  other arithmetic  17.5 us (2%)
  between operations  14.1 us (2%)
    all_to_all x1, waiting for transfers between devices, per_device(): lax.all_to_all(packed[0], 'dp', split_axis=0, concat_axis=0, tiled=True)  47.4 us
    all_to_all x1, waiting for transfers between devices, per_device(): lax.all_to_all(attn_out, 'dp', split_axis=0, concat_axis=0, tiled=True)  47.3 us
    all_to_all x1, waiting for transfers between devices, per_device(): lax.all_to_all(q_grad, 'dp', split_axis=0, concat_axis=0, tiled=True)  45.1 us
    dot_general x32, matrix products, attend_one(): jnp.einsum('qk,qd->kd', probs_low, g_head, preferred_element_type=jnp.flo...  43.7 us
    all_to_all x1, waiting for transfers between devices, per_device(): lax.all_to_all(packed[3], 'dp', split_axis=0, concat_axis=0, tiled=True)  43.2 us
    dot_general x32, matrix products, attend_one(): jnp.einsum('qk,qd->kd', score_grad, q_head, preferred_element_type=jnp.fl...  42.4 us
    dot_general x32, matrix products, attend_one(): jnp.einsum('qk,kd->qd', probs_low, v_head, preferred_element_type=jnp.flo...  41.2 us
    dot_general x32, matrix products, attend_one(): jnp.einsum('qd,kd->qk', g_head, v_head, preferred_element_type=jnp.float32)  38 us
  transfers between devices with their start and end apart: 12, of which 8 were waited for; matrix products, arithmetic and copies ran while one was open for 4% of the time, Pallas kernels for 0%

commit v1 on v0

v1 whole, which is shorter than its diff:
```python
import math

import jax
import jax.numpy as jnp
from jax import lax
from jax.experimental import pallas as pl
from jax.experimental.pallas import tpu as pltpu
from jax.sharding import PartitionSpec as P

HD = 128
NX, NZ, NS = 4, 8, 8
NG = NX * NS
CAP = 5
SLOTS = NG * CAP
HALF = SLOTS // 2
KEYS = NZ * SLOTS
HEADS, KVH, RATIO = 32, 8, 4
UNITS = 16
PIECES = 4
ROWS = 128
BLK = 16
MESH = pl.DeviceIdType.MESH
BF16 = jnp.bfloat16
F32 = jnp.float32
VMEM_LIMIT = 56 * 1024 * 1024


def iota(shape, dim):
    return lax.broadcasted_iota(jnp.int32, shape, dim)


def dot(a, b):
    return lax.dot_general(a, b, (((1,), (0,)), ((), ())), preferred_element_type=F32)


def dot_nt(a, b):
    return lax.dot_general(a, b, (((1,), (1,)), ((), ())), preferred_element_type=F32)


def place():
    dp, seq = lax.axis_index("dp"), lax.axis_index("seq")
    return dp // NZ, lax.rem(dp, NZ), seq


def plane_device(x, z, seq, step):
    to_x = lax.rem(x + step // NS, NX)
    rest = lax.rem(step, NS)
    to_y = lax.rem(seq // 2 + rest // 2, NS // 2)
    to_core = lax.rem(seq + rest, 2)
    to_seq = to_y * 2 + to_core
    return to_x * NS + to_seq, (to_x * NZ + z, to_seq)


def swap_matrix():
    row, col = iota((256, 256), 0), iota((256, 256), 1)
    return (col == lax.rem(row, 16) * 16 + row // 16).astype(BF16)


def slot_rows(group_ref):
    across = jnp.broadcast_to(group_ref[...], (ROWS, ROWS)).astype(F32)
    down = across.T
    earlier = (across == down) & (iota((ROWS, ROWS), 0) < iota((ROWS, ROWS), 1))
    rank = jnp.sum(earlier.astype(F32), axis=0, keepdims=True)
    return across[:1] * CAP + rank


def slot_matrix(group_ref):
    return (iota((SLOTS, ROWS), 0).astype(F32) == slot_rows(group_ref)).astype(BF16)


def swap_tiles(swap, tiles):
    mixed = dot(swap, jnp.concatenate(tiles, axis=0)).astype(BF16)
    return [mixed[i * 16 : (i + 1) * 16] for i in range(16)]


def greet(x, z, seq, ring):
    barrier = pltpu.get_barrier_semaphore()

    def signal(step, carry):
        _, device = plane_device(x, z, seq, step)
        pl.semaphore_signal(barrier, inc=1, device_id=device, device_id_type=MESH)
        return carry

    lax.fori_loop(1, NG, signal, 0)
    for device in ring:
        pl.semaphore_signal(barrier, inc=1, device_id=device, device_id_type=MESH)
    pl.semaphore_wait(barrier, NG - 1 + len(ring))


def exchange_start(x, z, seq, send, recv, send_sem, recv_sem, own_sem):
    me = x * NS + seq

    def one(step, carry):
        to, device = plane_device(x, z, seq, step)
        pltpu.make_async_remote_copy(
            src_ref=send.at[to],
            dst_ref=recv.at[me],
            send_sem=send_sem,
            recv_sem=recv_sem,
            device_id=device,
            device_id_type=MESH,
        ).start()
        return carry

    lax.fori_loop(1, NG, one, 0)
    pltpu.make_async_copy(send.at[me], recv.at[me], own_sem).start()


def exchange_wait_recv(recv, recv_sem, own_sem):
    pltpu.make_async_copy(recv.at[pl.ds(0, NG - 1)], recv.at[pl.ds(0, NG - 1)], recv_sem).wait()
    pltpu.make_async_copy(recv.at[0], recv.at[0], own_sem).wait()


def exchange_wait_send(send, send_sem):
    pltpu.make_async_copy(send.at[pl.ds(0, NG - 1)], send.at[pl.ds(0, NG - 1)], send_sem).wait()


def token_tiles(ref, base, block):
    tiles = []
    for t in range(block * BLK, block * BLK + BLK):
        tiles.append(ref[base + (t // CAP,) + (t % CAP,)])
    return tiles


def put_tiles(ref, base, block, tiles):
    for i, tile in enumerate(tiles):
        t = block * BLK + i
        ref[base + (t // CAP,) + (t % CAP,)] = tile


def spread_kernel(
    q_ref, k_ref, v_ref, g_ref, group_ref, doc_ref,
    kv_ref, meta_ref, qu_ref, gu_ref,
    send0, recv0, send, recv,
    s0, r0, o0, ss, rs, os, ring_s, ring_r, meta_s, meta_r,
):
    x, z, seq = place()
    me = x * NS + seq
    right = (x * NZ + lax.rem(z + 1, NZ), seq)
    left = (x * NZ + lax.rem(z + NZ - 1, NZ), seq)

    pick = slot_matrix(group_ref)
    swap = swap_matrix()

    def pack(into, base, parts):
        packed = [dot(pick, part).astype(BF16) for part in parts]
        for block in range(SLOTS // BLK):
            rows = slice(block * BLK, (block + 1) * BLK)
            tiles = []
            for unit in range(UNITS):
                src, at = packed[unit // (UNITS // len(parts))], unit % (UNITS // len(parts))
                tiles.append(src[rows, at * HD : (at + 1) * HD])
            put_tiles(into, base, block, swap_tiles(swap, tiles))

    pack(send0, (), [k_ref[...], v_ref[...]])
    code = dot_nt(pick, jnp.broadcast_to(doc_ref[...] + 1, (HD, ROWS)).astype(BF16))
    slot, lane = iota((SLOTS, HD), 0), iota((SLOTS, HD), 1)
    at_lane = lax.rem(me, 2) * CAP + lax.rem(slot, CAP)
    code = jnp.where(lane == at_lane, code, 0.0).astype(BF16)
    row, col = iota((NG * 16, SLOTS), 0), iota((NG * 16, SLOTS), 1)
    sel = ((row // 16 == col // CAP) & (lax.rem(row, 16) == me // 2)).astype(BF16)
    codes = dot(sel, code).astype(BF16)
    for d in range(NG):
        send0[d, CAP] = codes[d * 16 : (d + 1) * 16]

    greet(x, z, seq, (left, right))
    exchange_start(x, z, seq, send0, recv0, s0, r0, o0)

    for piece in range(PIECES):
        cols = slice(piece * 1024, (piece + 1) * 1024)
        pack(send, (piece,), [q_ref[:, cols], g_ref[:, cols]])
        exchange_start(
            x, z, seq, send.at[piece], recv.at[piece], ss.at[piece], rs.at[piece], os.at[piece]
        )

    exchange_wait_recv(recv0, r0, o0)
    here = pl.multiple_of(z * HALF, BLK)
    for block in range(SLOTS // BLK):
        tiles = swap_tiles(swap, token_tiles(recv0, (), block))
        half, at = block // 5, (block % 5) * BLK
        for unit in range(UNITS):
            kv_ref[unit % 8, unit // 8, half, pl.ds(here + at, BLK), :] = tiles[unit]
    total = recv0[0, CAP]
    for s in range(1, NG):
        total = total + recv0[s, CAP]
    meta_ref[z] = total

    def ring_copy(lane_id, step):
        goes_right = lane_id < 2
        owner = lax.rem(z - step + NZ, NZ) if goes_right else lax.rem(z + step, NZ)
        block = kv_ref.at[
            pl.ds(lane_id * 2, 2), :, :, pl.ds(pl.multiple_of(owner * HALF, BLK), HALF), :
        ]
        return pltpu.make_async_remote_copy(
            src_ref=block,
            dst_ref=block,
            send_sem=ring_s.at[lane_id, step],
            recv_sem=ring_r.at[lane_id, step],
            device_id=right if goes_right else left,
            device_id_type=MESH,
        )

    def meta_copy(step):
        owner = lax.rem(z - step + NZ, NZ)
        return pltpu.make_async_remote_copy(
            src_ref=meta_ref.at[owner],
            dst_ref=meta_ref.at[owner],
            send_sem=meta_s.at[step],
            recv_sem=meta_r.at[step],
            device_id=right,
            device_id_type=MESH,
        )

    def unpack(piece):
        exchange_wait_recv(recv.at[piece], rs.at[piece], os.at[piece])
        for block in range(SLOTS // BLK):
            tiles = swap_tiles(swap, token_tiles(recv, (piece,), block))
            rows = slice(block * BLK, (block + 1) * BLK)
            for unit in range(8):
                qu_ref[piece * 8 + unit, rows, :] = tiles[unit]
                gu_ref[piece * 8 + unit, rows, :] = tiles[8 + unit]

    for step in range(NZ - 1):
        for lane_id in (0, 2, 1, 3):
            if step > 0:
                ring_copy(lane_id, step - 1).wait_recv()
            ring_copy(lane_id, step).start()
        if step > 0:
            meta_copy(step - 1).wait_recv()
        meta_copy(step).start()
        if step >= 3:
            unpack(step - 3)
    for lane_id in range(4):
        ring_copy(lane_id, NZ - 2).wait_recv()
    meta_copy(NZ - 2).wait_recv()
    for step in range(NZ - 1):
        for lane_id in range(4):
            ring_copy(lane_id, step).wait_send()
        meta_copy(step).wait_send()
    exchange_wait_send(send0, s0)
    for piece in range(PIECES):
        exchange_wait_send(send.at[piece], ss.at[piece])


LANES = RATIO * SLOTS
SPLIT = 256


def mask_bias(meta_ref, bias):
    _, z, _ = place()
    t, b16 = iota((SLOTS, 16), 0), iota((SLOTS, 16), 1)
    spread = (t // 10 == b16).astype(BF16)
    t2, lane = iota((SLOTS, HD), 0), iota((SLOTS, HD), 1)
    ones = jnp.ones((HD, HD), BF16)
    lane_q = iota((HD, LANES), 1)
    tq = (lane_q // (RATIO * HALF)) * HALF + lax.rem(lane_q, HALF)
    expand = (iota((HD, LANES), 0) == lax.rem(tq, 10)).astype(BF16)
    wide = dot(meta_ref[z], expand)
    lane_q = iota((16, LANES), 1)
    tq = (lane_q // (RATIO * HALF)) * HALF + lax.rem(lane_q, HALF)
    code_q = jnp.sum(jnp.where(iota((16, LANES), 0) == tq // 10, wide, 0.0), axis=0, keepdims=True)
    tq = tq[:1]
    order_q = (tq // 40) * 320 + z * 40 + lax.rem(tq, 40)
    for zk in range(NZ):
        picked = dot(spread, meta_ref[zk])
        picked = jnp.where(lane == lax.rem(t2, 10), picked, 0.0).astype(BF16)
        code_k = dot(picked, ones)
        order_k = (t2 // 40) * 320 + zk * 40 + lax.rem(t2, 40)
        for half in range(2):
            rows = slice(half * HALF, (half + 1) * HALF)
            for at in range(0, LANES, HD):
                cols = slice(at, at + HD)
                ok = (
                    (code_k[rows] == code_q[:, cols])
                    & (code_k[rows] > 0.5)
                    & (order_k[rows] <= order_q[:, cols])
                )
                bias[pl.ds(half * NZ * HALF + zk * HALF, HALF), cols] = jnp.where(ok, 0.0, -1e30)


def attend_kernel(kv_ref, meta_ref, q_ref, g_ref, o_ref, dq_ref, dkv_ref, bias, p_ref, ds_ref):
    inv_root = 1.0 / math.sqrt(HD)
    log_scale = inv_root * math.log2(math.e)

    @pl.when(pl.program_id(0) == 0)
    def _():
        mask_bias(meta_ref, bias)

    def rows_of(ref):
        return jnp.concatenate(
            [ref[h, half * HALF : (half + 1) * HALF, :] for half in range(2) for h in range(RATIO)],
            axis=0,
        )

    q, g = rows_of(q_ref), rows_of(g_ref)
    k = kv_ref[0, 0].reshape(KEYS, HD)
    v = kv_ref[0, 1].reshape(KEYS, HD)
    kt, vt, gt = k.T, v.T, g.T
    outs, dqs = [], []
    for lo, hi, n in ((0, SPLIT, KEYS // 2), (SPLIT, 2 * SPLIT, KEYS), (2 * SPLIT, LANES, KEYS)):
        s = dot_nt(k[:n], q[lo:hi]) * log_scale + bias[:n, lo:hi]
        p = jnp.exp2(s - jnp.max(s, axis=0, keepdims=True))
        p = p * (1.0 / jnp.sum(p, axis=0, keepdims=True))
        low = p.astype(BF16)
        p_ref[:n, lo:hi] = low
        out = dot(vt[:, :n], low).astype(BF16)
        delta = jnp.sum(gt[:, lo:hi].astype(F32) * out.astype(F32), axis=0, keepdims=True)
        ds = (p * (dot_nt(v[:n], g[lo:hi]) - delta)).astype(BF16)
        ds_ref[:n, lo:hi] = ds
        outs.append(out.T)
        dqs.append((dot(kt[:, :n], ds) * inv_root).astype(BF16).T)
    out, dq = jnp.concatenate(outs, axis=0), jnp.concatenate(dqs, axis=0)
    for half in range(2):
        for h in range(RATIO):
            rows = slice((half * RATIO + h) * HALF, (half * RATIO + h + 1) * HALF)
            o_ref[h, half * HALF : (half + 1) * HALF, :] = out[rows]
            dq_ref[h, half * HALF : (half + 1) * HALF, :] = dq[rows]
    n = KEYS // 2
    for half, lo in ((0, 0), (1, SPLIT)):
        rows = slice(half * n, (half + 1) * n)
        dkv_ref[0, 0, half] = (dot(ds_ref[rows, lo:], q[lo:]) * inv_root).astype(BF16)
        dkv_ref[0, 1, half] = dot(p_ref[rows, lo:], g[lo:]).astype(BF16)


def collect_kernel(
    o_ref, dq_ref, dkv_ref, group_ref,
    out_ref, qg_ref, kg_ref, vg_ref,
    send0, recv0, send, recv, land, stage,
    s0, r0, o0, ss, rs, os, ring_s, ring_r,
):
    x, z, seq = place()
    right = (x * NZ + lax.rem(z + 1, NZ), seq)
    left = (x * NZ + lax.rem(z + NZ - 1, NZ), seq)
    pick_t = slot_matrix(group_ref).astype(F32).T.astype(BF16)
    swap = swap_matrix()
    greet(x, z, seq, (left, right))

    def own(lane_id, step):
        goes_right = lane_id < 2
        to = lax.rem(z - 1 - step + 2 * NZ, NZ) if goes_right else lax.rem(z + 1 + step, NZ)
        return dkv_ref[
            pl.ds(lane_id * 2, 2), :, :, pl.ds(pl.multiple_of(to * HALF, BLK), HALF), :
        ]

    def ring_copy(lane_id, step):
        return pltpu.make_async_remote_copy(
            src_ref=stage.at[lane_id, step],
            dst_ref=land.at[lane_id, step],
            send_sem=ring_s.at[lane_id, step],
            recv_sem=ring_r.at[lane_id, step],
            device_id=right if lane_id < 2 else left,
            device_id_type=MESH,
        )

    def summed(lane_id, step):
        return (
            own(lane_id, step).astype(F32) + land[lane_id, step - 1].astype(F32)
        ).astype(BF16)

    def pack(piece):
        for block in range(SLOTS // BLK):
            rows = slice(block * BLK, (block + 1) * BLK)
            tiles = [o_ref[piece * 8 + unit, rows, :] for unit in range(8)]
            tiles += [dq_ref[piece * 8 + unit, rows, :] for unit in range(8)]
            put_tiles(send, (piece,), block, swap_tiles(swap, tiles))
        exchange_start(
            x, z, seq, send.at[piece], recv.at[piece], ss.at[piece], rs.at[piece], os.at[piece]
        )

    def unpack(ref, base, outs):
        parts = [[] for _ in range(UNITS)]
        for block in range(SLOTS // BLK):
            tiles = swap_tiles(swap, token_tiles(ref, base, block))
            for unit in range(UNITS):
                parts[unit].append(tiles[unit])
        for unit in range(UNITS):
            rows = jnp.concatenate(parts[unit], axis=0)
            target, at = outs[unit // 8], unit % 8
            target[:, at * HD : (at + 1) * HD] = dot(pick_t, rows).astype(BF16)

    for step in range(NZ - 1):
        for lane_id in (0, 2, 1, 3):
            if step > 0:
                ring_copy(lane_id, step - 1).wait_recv()
                stage[lane_id, step] = summed(lane_id, step)
            else:
                stage[lane_id, step] = own(lane_id, step)
            ring_copy(lane_id, step).start()
        if step < PIECES:
            pack(step)
    for lane_id in range(4):
        ring_copy(lane_id, NZ - 2).wait_recv()
        stage[lane_id, NZ - 1] = summed(lane_id, NZ - 1)
    for block in range(SLOTS // BLK):
        half, at = block // 5, (block % 5) * BLK
        tiles = []
        for unit in range(UNITS):
            head, which = unit % 8, unit // 8
            tiles.append(stage[head // 2, NZ - 1, head % 2, which, half, at : at + BLK, :])
        put_tiles(send0, (), block, swap_tiles(swap, tiles))
    exchange_start(x, z, seq, send0, recv0, s0, r0, o0)
    for piece in range(PIECES):
        exchange_wait_recv(recv.at[piece], rs.at[piece], os.at[piece])
        cols = pl.ds(piece * 1024, 1024)
        unpack(recv, (piece,), [out_ref.at[:, cols], qg_ref.at[:, cols]])
    exchange_wait_recv(recv0, r0, o0)
    unpack(recv0, (), [kg_ref, vg_ref])
    for step in range(NZ - 1):
        for lane_id in range(4):
            ring_copy(lane_id, step).wait_send()
    exchange_wait_send(send0, s0)
    for piece in range(PIECES):
        exchange_wait_send(send.at[piece], ss.at[piece])


def per_device(query, key_states, value_states, out_grad, target_group, document):
    vmem = pl.BlockSpec(memory_space=pltpu.VMEM)
    dma = pltpu.SemaphoreType.DMA
    group = target_group.reshape(1, ROWS)
    doc = document.reshape(1, ROWS)
    kv_shape = (KVH, 2, 2, NZ * HALF, HD)
    kv, meta, qu, gu = pl.pallas_call(
        spread_kernel,
        out_shape=[
            jax.ShapeDtypeStruct(kv_shape, BF16),
            jax.ShapeDtypeStruct((NZ, 16, HD), BF16),
            jax.ShapeDtypeStruct((HEADS, SLOTS, HD), BF16),
            jax.ShapeDtypeStruct((HEADS, SLOTS, HD), BF16),
        ],
        in_specs=[vmem] * 6,
        out_specs=[vmem] * 4,
        scratch_shapes=[
            pltpu.VMEM((NG, CAP + 1, UNITS, HD), BF16),
            pltpu.VMEM((NG, CAP + 1, UNITS, HD), BF16),
            pltpu.VMEM((PIECES, NG, CAP, UNITS, HD), BF16),
            pltpu.VMEM((PIECES, NG, CAP, UNITS, HD), BF16),
            dma, dma, dma,
            dma((PIECES,)), dma((PIECES,)), dma((PIECES,)),
            dma((4, NZ - 1)), dma((4, NZ - 1)),
            dma((NZ - 1,)), dma((NZ - 1,)),
        ],
        compiler_params=pltpu.CompilerParams(
            collective_id=0, has_side_effects=True, vmem_limit_bytes=VMEM_LIMIT
        ),
        name="spread",
    )(query, key_states, value_states, out_grad, group, doc)

    heads = pl.BlockSpec((RATIO, SLOTS, HD), lambda c: (c, 0, 0))
    kv_block = pl.BlockSpec((1, 2, 2, NZ * HALF, HD), lambda c: (c, 0, 0, 0, 0))
    out, dq, dkv = pl.pallas_call(
        attend_kernel,
        grid=(KVH,),
        out_shape=[
            jax.ShapeDtypeStruct((HEADS, SLOTS, HD), BF16),
            jax.ShapeDtypeStruct((HEADS, SLOTS, HD), BF16),
            jax.ShapeDtypeStruct(kv_shape, BF16),
        ],
        in_specs=[kv_block, pl.BlockSpec((NZ, 16, HD), lambda c: (0, 0, 0)), heads, heads],
        out_specs=[heads, heads, kv_block],
        scratch_shapes=[
            pltpu.VMEM((KEYS, LANES), F32),
            pltpu.VMEM((KEYS, LANES), BF16),
            pltpu.VMEM((KEYS, LANES), BF16),
        ],
        compiler_params=pltpu.CompilerParams(vmem_limit_bytes=VMEM_LIMIT),
        name="attend",
    )(kv, meta, qu, gu)

    return tuple(
        pl.pallas_call(
            collect_kernel,
            out_shape=[
                jax.ShapeDtypeStruct((ROWS, HEADS * HD), BF16),
                jax.ShapeDtypeStruct((ROWS, HEADS * HD), BF16),
                jax.ShapeDtypeStruct((ROWS, KVH * HD), BF16),
                jax.ShapeDtypeStruct((ROWS, KVH * HD), BF16),
            ],
            in_specs=[vmem] * 4,
            out_specs=[vmem] * 4,
            scratch_shapes=[
                pltpu.VMEM((NG, CAP, UNITS, HD), BF16),
                pltpu.VMEM((NG, CAP, UNITS, HD), BF16),
                pltpu.VMEM((PIECES, NG, CAP, UNITS, HD), BF16),
                pltpu.VMEM((PIECES, NG, CAP, UNITS, HD), BF16),
                pltpu.VMEM((4, NZ - 1, 2, 2, 2, HALF, HD), BF16),
                pltpu.VMEM((4, NZ, 2, 2, 2, HALF, HD), BF16),
                dma, dma, dma,
                dma((PIECES,)), dma((PIECES,)), dma((PIECES,)),
                dma((4, NZ - 1)), dma((4, NZ - 1)),
            ],
            compiler_params=pltpu.CompilerParams(
                collective_id=1, has_side_effects=True, vmem_limit_bytes=VMEM_LIMIT
            ),
            name="collect",
        )(out, dq, dkv, group)
    )


def solution(mesh):
    rows = P(("dp", "seq"), None)
    line = P(("dp", "seq"))
    return jax.shard_map(
        per_device,
        mesh=mesh,
        in_specs=(rows, rows, rows, rows, line, line),
        out_specs=(rows, rows, rows, rows),
        check_vma=False,
    )
```

time: 717 us -> 201 us (0.28); the launches traced: 705 us -> 199 us
  waiting for transfers between devices: 223 us -> 0 us
  matrix products: 212 us -> 0 us
  Pallas kernels: 0 us -> 193 us
  local copies, waits for them, and re-layouts: 117 us -> 4.88 us
  starting transfers between devices: 45.3 us -> 0 us
  blocking collectives: 43.1 us -> 0 us
  loops' own time: 33.3 us -> 0 us
  other arithmetic: 17.5 us -> 0 us
  between operations: 14.1 us -> 0.66 us
    all_to_all x8 -> x0, waiting for transfers between devices: 222 us -> none  [the longest x1 47.4 us: per_device(): lax.all_to_all(packed[0], 'dp', split_axis=0, concat_axis=0, tiled=True)]
    dot_general x192 -> x0, matrix products: 212 us -> none  [the longest x32 43.7 us: attend_one(): jnp.einsum('qk,qd->kd', probs_low, g_head, preferred_element_type=jnp.flo...]
    pallas_call x0 -> x3, Pallas kernels: none -> 193 us  [the longest x1 79.5 us: per_device(): pl.pallas_call(spread_kernel, out_shape=[jax.ShapeDtypeStruct(kv_shape, B...]
    all_to_all x8 -> x0, starting transfers between devices: 45 us -> none  [the longest x1 7.11 us: per_device(): lax.all_to_all(packed[0], 'dp', split_axis=0, concat_axis=0, tiled=True)]
    all_to_all x2 -> x0, blocking collectives: 43.1 us -> none  [the longest x1 28.7 us: per_device(): lax.all_to_all(packed[1], 'dp', split_axis=0, concat_axis=0, tiled=True)]
    dynamic_slice x56 -> x0, local copies, waits for them, and re-layouts: 40.5 us -> none  [the longest x32 19.8 us: per_kv(): lax.scan(per_query_head, (zero_grad, zero_grad), jnp.arange(head_ratio, d...]
    another operation x9 -> x0, loops' own time: 33.3 us -> none  [the longest x8 22.2 us: per_kv(): lax.scan(per_query_head, (zero_grad, zero_grad), jnp.arange(head_ratio, d...]
    all_to_all x22 -> x0, local copies, waits for them, and re-layouts: 22.3 us -> none  [the longest x2 4.3 us: per_device(): lax.all_to_all(attn_out, 'dp', split_axis=0, concat_axis=0, tiled=True)]
  transfers between devices with their start and end apart: 12 -> 0, of which waited for: 8 -> 0; matrix products, arithmetic and copies ran while one was open for 4% -> 0% of each run, Pallas kernels for 0% -> 0%
where the time goes in v1:
time: 201 us; the launch traced here: 199 us
  Pallas kernels  193 us (96%)
  local copies, waits for them, and re-layouts  4.88 us (2%)
    pallas_call x1, Pallas kernels, per_device(): pl.pallas_call(spread_kernel, out_shape=[jax.ShapeDtypeStruct(kv_shape, B...  79.5 us
    pallas_call x1, Pallas kernels, per_device(): pl.pallas_call(collect_kernel, out_shape=[jax.ShapeDtypeStruct((ROWS, HEA...  74.9 us
    pallas_call x1, Pallas kernels, per_device(): pl.pallas_call(attend_kernel, grid=(KVH,), out_shape=[jax.ShapeDtypeStruc...  39 us
    unnamed x10, local copies, waits for them, and re-layouts  4.88 us

profile of v1, /device:TPU:32, one launch (start us, length us, event | category | flops | bytes accessed | tf_op | source)
XLA Modules:
  0.0 198.9 jit_solution(12871414138389933123)
XLA Ops:
  0.6 79.5 %spread.1 = (bf16[8,2,2,640,128]{4,3,2,1,0:T(8,128)(2,1)}, bf16[8,16,128]{2,1,0:T(8,128)(2,1)}, bf16[32,160,128]{2,1,0:T(8,128)(2,1)}, bf16[32,160,128]{2,1,0:T(8,128)(2,1)}) custom-call(bf16[128,4096]{1,0:T(8,128)(2,1)} %q_ref.1, bf16[128,1024]{1,0:T(8,128)(2,1)} %k_ref.1, bf16[128,1024]{1,0:T(8,128)(2,1)} %v_ref.1, bf16[128,4096]{1,0:T(8,128)(2,1)} %g_ref.1, ...), custom_call_target="tpu_custom_call" | custom-call | tf_op jit(solution)/shard_map/spread/pallas_call | solution.py:422
  80.1 39.0 %attend.1 = (bf16[32,160,128]{2,1,0:T(8,128)(2,1)}, bf16[32,160,128]{2,1,0:T(8,128)(2,1)}, bf16[8,2,2,640,128]{4,3,2,1,0:T(8,128)(2,1)}) custom-call(bf16[8,2,2,640,128]{4,3,2,1,0:T(8,128)(2,1)} %get-tuple-element.11.kv_ref, bf16[8,16,128]{2,1,0:T(8,128)(2,1)} %get-tuple-element.12.meta_ref, bf16[32,160,128]{2,1,0:T(8,128)(2,1)} %get-tuple-element.13.q_ref, ...), custom_call_target="tpu_custom_call" | custom-call | tf_op jit(solution)/shard_map/attend/pallas_call | solution.py:450
  119.1 74.9 %collect.1 = (bf16[128,4096]{1,0:T(8,128)(2,1)}, bf16[128,4096]{1,0:T(8,128)(2,1)}, bf16[128,1024]{1,0:T(8,128)(2,1)}, bf16[128,1024]{1,0:T(8,128)(2,1)}) custom-call(bf16[32,160,128]{2,1,0:T(8,128)(2,1)} %get-tuple-element.15.o_ref, bf16[32,160,128]{2,1,0:T(8,128)(2,1)} %get-tuple-element.16.dq_ref, bf16[8,2,2,640,128]{4,3,2,1,0:T(8,128)(2,1)} %get-tuple-element.17.dkv_ref, ...), custom_call_target="tpu_custom_call" | custom-call | tf_op jit(solution)/shard_map/collect/pallas_call | solution.py:470
  194.0 0.0 copy-start
  194.0 2.4 %copy.14 = bf16[128,4096]{1,0:T(8,128)(2,1)} copy(bf16[128,4096]{1,0:T(8,128)(2,1)} %get-tuple-element.22) | data formatting | bytes 2097152
  196.4 0.0 copy-done
  196.4 0.0 copy-start.2
  196.4 0.0 copy-start.1
  196.4 1.0 copy.15
  197.4 0.1 copy-done.2
  197.5 0.7 copy.16
  198.2 0.0 copy-done.1
  198.2 0.7 copy.17
Async XLA Ops:
  194.0 2.4 %copy-start = (bf16[128,4096]{1,0:T(8,128)(2,1)S(1)}, bf16[128,4096]{1,0:T(8,128)(2,1)}, u32[]{:S(2)}) copy-start(bf16[128,4096]{1,0:T(8,128)(2,1)} %get-tuple-element.23) | copy-start | bytes 3145732
  196.4 1.1 copy-start.2
  196.4 1.8 copy-start.1

commit v2 on v1

v2 whole, which is shorter than its diff:
```python
import math

import jax
import jax.numpy as jnp
from jax import lax
from jax.experimental import pallas as pl
from jax.experimental.pallas import tpu as pltpu
from jax.sharding import PartitionSpec as P

HD = 128
NX, NZ, NS = 4, 8, 8
NG = NX * NS
CAP = 5
SLOTS = NG * CAP
HALF = SLOTS // 2
KEYS = NZ * SLOTS
HEADS, KVH, RATIO = 32, 8, 4
UNITS = 16
PIECES = 4
ROWS = 128
BLK = 16
MESH = pl.DeviceIdType.MESH
BF16 = jnp.bfloat16
F32 = jnp.float32
VMEM_LIMIT = 56 * 1024 * 1024


def iota(shape, dim):
    return lax.broadcasted_iota(jnp.int32, shape, dim)


def dot(a, b):
    return lax.dot_general(a, b, (((1,), (0,)), ((), ())), preferred_element_type=F32)


def dot_nt(a, b):
    return lax.dot_general(a, b, (((1,), (1,)), ((), ())), preferred_element_type=F32)


def place():
    dp, seq = lax.axis_index("dp"), lax.axis_index("seq")
    return dp // NZ, lax.rem(dp, NZ), seq


def plane_device(x, z, seq, step):
    to_x = lax.rem(x + step // NS, NX)
    rest = lax.rem(step, NS)
    to_y = lax.rem(seq // 2 + rest // 2, NS // 2)
    to_core = lax.rem(seq + rest, 2)
    to_seq = to_y * 2 + to_core
    return to_x * NS + to_seq, (to_x * NZ + z, to_seq)


def swap_matrix():
    row, col = iota((256, 256), 0), iota((256, 256), 1)
    return (col == lax.rem(row, 16) * 16 + row // 16).astype(BF16)


def slot_rows(group_ref):
    across = jnp.broadcast_to(group_ref[...], (ROWS, ROWS)).astype(F32)
    down = across.T
    earlier = (across == down) & (iota((ROWS, ROWS), 0) < iota((ROWS, ROWS), 1))
    rank = jnp.sum(earlier.astype(F32), axis=0, keepdims=True)
    return across[:1] * CAP + rank


def slot_matrix(group_ref):
    return (iota((SLOTS, ROWS), 0).astype(F32) == slot_rows(group_ref)).astype(BF16)


def swap_tiles(swap, tiles):
    mixed = dot(swap, jnp.concatenate(tiles, axis=0)).astype(BF16)
    return [mixed[i * 16 : (i + 1) * 16] for i in range(16)]


def greet(x, z, seq, ring):
    barrier = pltpu.get_barrier_semaphore()

    def signal(step, carry):
        _, device = plane_device(x, z, seq, step)
        pl.semaphore_signal(barrier, inc=1, device_id=device, device_id_type=MESH)
        return carry

    lax.fori_loop(1, NG, signal, 0)
    for device in ring:
        pl.semaphore_signal(barrier, inc=1, device_id=device, device_id_type=MESH)
    pl.semaphore_wait(barrier, NG - 1 + len(ring))


def exchange_start(x, z, seq, send, recv, send_sem, recv_sem, own_sem):
    me = x * NS + seq

    def one(step, carry):
        to, device = plane_device(x, z, seq, step)
        pltpu.make_async_remote_copy(
            src_ref=send.at[to],
            dst_ref=recv.at[me],
            send_sem=send_sem,
            recv_sem=recv_sem,
            device_id=device,
            device_id_type=MESH,
        ).start()
        return carry

    lax.fori_loop(1, NG, one, 0)
    pltpu.make_async_copy(send.at[me], recv.at[me], own_sem).start()


def exchange_wait_recv(recv, recv_sem, own_sem):
    pltpu.make_async_copy(recv.at[pl.ds(0, NG - 1)], recv.at[pl.ds(0, NG - 1)], recv_sem).wait()
    pltpu.make_async_copy(recv.at[0], recv.at[0], own_sem).wait()


def exchange_wait_send(send, send_sem):
    pltpu.make_async_copy(send.at[pl.ds(0, NG - 1)], send.at[pl.ds(0, NG - 1)], send_sem).wait()


def token_tiles(ref, base, block):
    tiles = []
    for t in range(block * BLK, block * BLK + BLK):
        tiles.append(ref[base + (t // CAP,) + (t % CAP,)])
    return tiles


def put_tiles(ref, base, block, tiles):
    for i, tile in enumerate(tiles):
        t = block * BLK + i
        ref[base + (t // CAP,) + (t % CAP,)] = tile


LANES = RATIO * SLOTS
SPLIT = 256
SET = KVH // 2
INV_ROOT = 1.0 / math.sqrt(HD)


def query_slots(rows):
    lane = iota((rows, LANES), 1)
    return (lane // (RATIO * HALF)) * HALF + lax.rem(lane, HALF)


def query_codes(meta):
    expand = (iota((HD, LANES), 0) == lax.rem(query_slots(HD), 10)).astype(BF16)
    own = iota((16, LANES), 0) == query_slots(16) // 10
    return jnp.sum(jnp.where(own, dot(meta, expand), 0.0), axis=0, keepdims=True)


def mask_block(meta_ref, bias, z, zk):
    tq = query_slots(1)
    code_q = query_codes(meta_ref[z])
    order_q = (tq // 40) * 320 + z * 40 + lax.rem(tq, 40)
    slot, lane = iota((SLOTS, HD), 0), iota((SLOTS, HD), 1)
    spread = (iota((SLOTS, 16), 0) // 10 == iota((SLOTS, 16), 1)).astype(BF16)
    picked = jnp.where(lane == lax.rem(slot, 10), dot(spread, meta_ref[zk]), 0.0).astype(BF16)
    code_k = dot(picked, jnp.ones((HD, HD), BF16))
    order_k = (slot // 40) * 320 + zk * 40 + lax.rem(slot, 40)
    for half in range(2):
        rows = slice(half * HALF, (half + 1) * HALF)
        at_row = pl.multiple_of(half * NZ * HALF + zk * HALF, BLK)
        for at in range(0, LANES, HD):
            cols = slice(at, at + HD)
            ok = (
                (code_k[rows] == code_q[:, cols])
                & (code_k[rows] > 0.5)
                & (order_k[rows] <= order_q[:, cols])
            )
            bias[pl.ds(at_row, HALF), cols] = jnp.where(ok, 0.0, -1e30)


def attend_head(c, kv_ref, q_ref, g_ref, o_ref, dq_ref, dkv_ref, bias, p_ref, ds_ref, between):
    log_scale = INV_ROOT * math.log2(math.e)

    def rows_of(ref):
        return jnp.concatenate(
            [
                ref[c * RATIO + h, half * HALF : (half + 1) * HALF, :]
                for half in range(2)
                for h in range(RATIO)
            ],
            axis=0,
        )

    q, g = rows_of(q_ref), rows_of(g_ref)
    k = kv_ref[c, 0].reshape(KEYS, HD)
    v = kv_ref[c, 1].reshape(KEYS, HD)
    kt, vt, gt = k.T, v.T, g.T
    outs, dqs = [], []
    blocks = ((0, SPLIT, KEYS // 2), (SPLIT, 2 * SPLIT, KEYS), (2 * SPLIT, LANES, KEYS))
    for i, (lo, hi, n) in enumerate(blocks):
        s = dot_nt(k[:n], q[lo:hi]) * log_scale + bias[:n, lo:hi]
        p = jnp.exp2(s - jnp.max(s, axis=0, keepdims=True))
        p = p * (1.0 / jnp.sum(p, axis=0, keepdims=True))
        low = p.astype(BF16)
        p_ref[:n, lo:hi] = low
        out = dot(vt[:, :n], low).astype(BF16)
        delta = jnp.sum(gt[:, lo:hi].astype(F32) * out.astype(F32), axis=0, keepdims=True)
        ds = (p * (dot_nt(v[:n], g[lo:hi]) - delta)).astype(BF16)
        ds_ref[:n, lo:hi] = ds
        outs.append(out.T)
        dqs.append((dot(kt[:, :n], ds) * INV_ROOT).astype(BF16).T)
        between(i)
    out, dq = jnp.concatenate(outs, axis=0), jnp.concatenate(dqs, axis=0)
    for half in range(2):
        for h in range(RATIO):
            rows = slice((half * RATIO + h) * HALF, (half * RATIO + h + 1) * HALF)
            o_ref[c * RATIO + h, half * HALF : (half + 1) * HALF, :] = out[rows]
            dq_ref[c * RATIO + h, half * HALF : (half + 1) * HALF, :] = dq[rows]
    n = KEYS // 2
    for half, lo in ((0, 0), (1, SPLIT)):
        rows = slice(half * n, (half + 1) * n)
        dkv_ref[c, 0, half] = (dot(ds_ref[rows, lo:], q[lo:]) * INV_ROOT).astype(BF16)
        dkv_ref[c, 1, half] = dot(p_ref[rows, lo:], g[lo:]).astype(BF16)
    between(3)


def whole_kernel(
    q_ref, k_ref, v_ref, g_ref, group_ref, doc_ref,
    out_ref, qg_ref, kg_ref, vg_ref,
    kv_ref, meta_ref, qu_ref, gu_ref, ou_ref, dqu_ref, dkv_ref,
    bias, p_ref, ds_ref,
    send0, recv0, send, recv, dkv_send, back0, back, land,
    kv_s, kv_r, kv_o, row_s, row_r, row_o, dkv_s, dkv_r, dkv_o, res_s, res_r, res_o,
    ring_s, ring_r, sum_s, sum_r, meta_s, meta_r,
):
    x, z, seq = place()
    me = x * NS + seq
    right = (x * NZ + lax.rem(z + 1, NZ), seq)
    left = (x * NZ + lax.rem(z + NZ - 1, NZ), seq)

    pick = slot_matrix(group_ref)
    swap = swap_matrix()

    def pack_rows(into, base, parts):
        packed = [dot(pick, part).astype(BF16) for part in parts]
        for block in range(SLOTS // BLK):
            rows = slice(block * BLK, (block + 1) * BLK)
            tiles = []
            for unit in range(UNITS):
                src, at = packed[unit // 8], unit % 8
                tiles.append(src[rows, at * HD : (at + 1) * HD])
            put_tiles(into, base, block, swap_tiles(swap, tiles))

    def rows_start(piece):
        exchange_start(
            x, z, seq, send.at[piece], recv.at[piece],
            row_s.at[piece], row_r.at[piece], row_o.at[piece],
        )

    def rows_unpack(piece):
        exchange_wait_recv(recv.at[piece], row_r.at[piece], row_o.at[piece])
        for block in range(SLOTS // BLK):
            tiles = swap_tiles(swap, token_tiles(recv, (piece,), block))
            rows = slice(block * BLK, (block + 1) * BLK)
            for unit in range(8):
                qu_ref[piece * 8 + unit, rows, :] = tiles[unit]
                gu_ref[piece * 8 + unit, rows, :] = tiles[8 + unit]

    def results_start(piece):
        exchange_wait_send(send.at[piece], row_s.at[piece])
        for block in range(SLOTS // BLK):
            rows = slice(block * BLK, (block + 1) * BLK)
            tiles = [ou_ref[piece * 8 + unit, rows, :] for unit in range(8)]
            tiles += [dqu_ref[piece * 8 + unit, rows, :] for unit in range(8)]
            put_tiles(send, (piece,), block, swap_tiles(swap, tiles))
        exchange_start(
            x, z, seq, send.at[piece], back.at[piece],
            res_s.at[piece], res_r.at[piece], res_o.at[piece],
        )

    def unpack_back(ref, base, outs):
        parts = [[] for _ in range(UNITS)]
        for block in range(SLOTS // BLK):
            tiles = swap_tiles(swap, token_tiles(ref, base, block))
            for unit in range(UNITS):
                parts[unit].append(tiles[unit])
        for unit in range(UNITS):
            rows = jnp.concatenate(parts[unit], axis=0)
            target, at = outs[unit // 8], unit % 8
            target[:, at * HD : (at + 1) * HD] = dot(pick_t, rows).astype(BF16)

    def results_unpack(piece):
        exchange_wait_recv(back.at[piece], res_r.at[piece], res_o.at[piece])
        cols = pl.ds(piece * 1024, 1024)
        unpack_back(back, (piece,), [out_ref.at[:, cols], qg_ref.at[:, cols]])

    def plane(index):
        return pl.ds(pl.multiple_of(index * HALF, BLK), HALF)

    def gather_copy(first, lane, step):
        owner = lax.rem(z - step + NZ, NZ) if lane < 2 else lax.rem(z + step, NZ)
        block = kv_ref.at[first + lane, :, :, plane(owner), :]
        return pltpu.make_async_remote_copy(
            src_ref=block,
            dst_ref=block,
            send_sem=ring_s.at[first + lane, step],
            recv_sem=ring_r.at[first + lane, step],
            device_id=right if lane < 2 else left,
            device_id_type=MESH,
        )

    def meta_copy(step):
        owner = lax.rem(z - step + NZ, NZ)
        return pltpu.make_async_remote_copy(
            src_ref=meta_ref.at[owner],
            dst_ref=meta_ref.at[owner],
            send_sem=meta_s.at[step],
            recv_sem=meta_r.at[step],
            device_id=right,
            device_id_type=MESH,
        )

    def own_terms(lane, step):
        return plane(lax.rem(z - 1 - step + 2 * NZ, NZ) if lane < 2 else lax.rem(z + 1 + step, NZ))

    def sum_copy(first, lane, step, src):
        return pltpu.make_async_remote_copy(
            src_ref=src,
            dst_ref=land.at[first + lane, step],
            send_sem=sum_s.at[first + lane, step],
            recv_sem=sum_r.at[first + lane, step],
            device_id=right if lane < 2 else left,
            device_id_type=MESH,
        )

    def sum_first(first):
        for lane in (0, 2, 1, 3):
            src = dkv_ref.at[first + lane, :, :, own_terms(lane, 0), :]
            sum_copy(first, lane, 0, src).start()

    def sum_next(first, lane, step, send_on):
        slot = land.at[first + lane, step - 1]
        sum_copy(first, lane, step - 1, slot).wait_recv()
        own = dkv_ref[first + lane, :, :, own_terms(lane, step), :]
        slot[...] = (own.astype(F32) + slot[...].astype(F32)).astype(BF16)
        if send_on:
            sum_copy(first, lane, step, slot).start()

    pack_rows(send0, (), [k_ref[...], v_ref[...]])
    code = dot_nt(pick, jnp.broadcast_to(doc_ref[...] + 1, (HD, ROWS)).astype(BF16))
    slot, lane = iota((SLOTS, HD), 0), iota((SLOTS, HD), 1)
    code = jnp.where(lane == lax.rem(me, 2) * CAP + lax.rem(slot, CAP), code, 0.0).astype(BF16)
    row, col = iota((NG * 16, SLOTS), 0), iota((NG * 16, SLOTS), 1)
    sel = ((row // 16 == col // CAP) & (lax.rem(row, 16) == me // 2)).astype(BF16)
    codes = dot(sel, code).astype(BF16)
    for d in range(NG):
        send0[d, CAP] = codes[d * 16 : (d + 1) * 16]

    greet(x, z, seq, (left, right))
    exchange_start(x, z, seq, send0, recv0, kv_s, kv_r, kv_o)
    for piece in range(PIECES):
        cols = slice(piece * 1024, (piece + 1) * 1024)
        pack_rows(send, (piece,), [q_ref[:, cols], g_ref[:, cols]])

    exchange_wait_recv(recv0, kv_r, kv_o)
    here = pl.multiple_of(z * HALF, BLK)
    for block in range(SLOTS // BLK):
        tiles = swap_tiles(swap, token_tiles(recv0, (), block))
        half, at = block // 5, (block % 5) * BLK
        for unit in range(UNITS):
            kv_ref[unit % 8, unit // 8, half, pl.ds(here + at, BLK), :] = tiles[unit]
    total = recv0[0, CAP]
    for s in range(1, NG):
        total = total + recv0[s, CAP]
    meta_ref[z] = total

    for step in range(NZ - 1):
        for lane in (0, 2, 1, 3):
            if step > 0:
                gather_copy(0, lane, step - 1).wait_recv()
            gather_copy(0, lane, step).start()
        if step > 0:
            meta_copy(step - 1).wait_recv()
        meta_copy(step).start()
        if step < PIECES:
            rows_start(step)
        mask_block(meta_ref, bias, z, lax.rem(z - step + NZ, NZ))
        if step >= 5:
            rows_unpack(step - 5)
    for lane in (0, 2, 1, 3):
        gather_copy(SET, lane, 0).start()
    meta_copy(NZ - 2).wait_recv()
    mask_block(meta_ref, bias, z, lax.rem(z + 1, NZ))
    for lane in (0, 2, 1, 3):
        gather_copy(0, lane, NZ - 2).wait_recv()

    refs = (kv_ref, qu_ref, gu_ref, ou_ref, dqu_ref, dkv_ref, bias, p_ref, ds_ref)

    def first_heads(i, carry):
        def between(at):
            step = 2 * i + 1 + at // 2
            for lane in ((0, 2), (1, 3))[at % 2]:

                @pl.when(step < NZ)
                def _():
                    gather_copy(SET, lane, step - 1).wait_recv()

                @pl.when(step < NZ - 1)
                def _():
                    gather_copy(SET, lane, step).start()

        attend_head(i, *refs, between)
        return carry

    lax.fori_loop(0, SET, first_heads, 0)
    sum_first(0)
    for piece in (0, 1):
        results_start(piece)
    for piece in (2, 3):
        rows_unpack(piece)

    def other_heads(i, carry):
        def between(at):
            step = 2 * i + 1 + at // 2
            for lane in ((0, 2), (1, 3))[at % 2]:

                @pl.when(step < NZ - 1)
                def _():
                    sum_next(0, lane, step, True)

                @pl.when(step == NZ - 1)
                def _():
                    sum_next(0, lane, step, False)

        attend_head(i + SET, *refs, between)
        return carry

    lax.fori_loop(0, SET, other_heads, 0)
    sum_first(SET)
    for piece in (2, 3):
        results_start(piece)
    pick_t = pick.astype(F32).T.astype(BF16)
    for step in range(1, NZ):
        for lane in (0, 2, 1, 3):
            sum_next(SET, lane, step, step < NZ - 1)
        if step in (2, 4):
            results_unpack(step // 2 - 1)
    for block in range(SLOTS // BLK):
        half, at = block // 5, (block % 5) * BLK
        tiles = [
            land[unit % 8, NZ - 2, unit // 8, half, at : at + BLK, :] for unit in range(UNITS)
        ]
        for i, tile in enumerate(swap_tiles(swap, tiles)):
            t = block * BLK + i
            dkv_send[t // CAP, t % CAP] = tile
    exchange_start(x, z, seq, dkv_send, back0, dkv_s, dkv_r, dkv_o)
    for piece in (2, 3):
        results_unpack(piece)
    exchange_wait_recv(back0, dkv_r, dkv_o)
    unpack_back(back0, (), [kg_ref, vg_ref])

    for step in range(NZ - 1):
        for lane in range(4):
            for first in (0, SET):
                gather_copy(first, lane, step).wait_send()
                sum_copy(first, lane, step, land.at[first + lane, step]).wait_send()
        meta_copy(step).wait_send()
    exchange_wait_send(send0, kv_s)
    exchange_wait_send(dkv_send, dkv_s)
    for piece in range(PIECES):
        exchange_wait_send(send.at[piece], res_s.at[piece])


def per_device(query, key_states, value_states, out_grad, target_group, document):
    vmem = pl.BlockSpec(memory_space=pltpu.VMEM)
    dma = pltpu.SemaphoreType.DMA
    group = target_group.reshape(1, ROWS)
    doc = document.reshape(1, ROWS)
    kv_shape = (KVH, 2, 2, NZ * HALF, HD)
    heads_shape = (HEADS, SLOTS, HD)
    piece_shape = (PIECES, NG, CAP, UNITS, HD)
    result = pl.pallas_call(
        whole_kernel,
        out_shape=[
            jax.ShapeDtypeStruct((ROWS, HEADS * HD), BF16),
            jax.ShapeDtypeStruct((ROWS, HEADS * HD), BF16),
            jax.ShapeDtypeStruct((ROWS, KVH * HD), BF16),
            jax.ShapeDtypeStruct((ROWS, KVH * HD), BF16),
        ],
        in_specs=[vmem] * 6,
        out_specs=[vmem] * 4,
        scratch_shapes=[
            pltpu.VMEM(kv_shape, BF16),
            pltpu.VMEM((NZ, 16, HD), BF16),
            pltpu.VMEM(heads_shape, BF16),
            pltpu.VMEM(heads_shape, BF16),
            pltpu.VMEM(heads_shape, BF16),
            pltpu.VMEM(heads_shape, BF16),
            pltpu.VMEM(kv_shape, BF16),
            pltpu.VMEM((KEYS, LANES), F32),
            pltpu.VMEM((KEYS, LANES), BF16),
            pltpu.VMEM((KEYS, LANES), BF16),
            pltpu.VMEM((NG, CAP + 1, UNITS, HD), BF16),
            pltpu.VMEM((NG, CAP + 1, UNITS, HD), BF16),
            pltpu.VMEM(piece_shape, BF16),
            pltpu.VMEM(piece_shape, BF16),
            pltpu.VMEM((NG, CAP, UNITS, HD), BF16),
            pltpu.VMEM((NG, CAP, UNITS, HD), BF16),
            pltpu.VMEM(piece_shape, BF16),
            pltpu.VMEM((KVH, NZ - 1, 2, 2, HALF, HD), BF16),
            dma, dma, dma,
            dma((PIECES,)), dma((PIECES,)), dma((PIECES,)),
            dma, dma, dma,
            dma((PIECES,)), dma((PIECES,)), dma((PIECES,)),
            dma((KVH, NZ - 1)), dma((KVH, NZ - 1)),
            dma((KVH, NZ - 1)), dma((KVH, NZ - 1)),
            dma((NZ - 1,)), dma((NZ - 1,)),
        ],
        compiler_params=pltpu.CompilerParams(
            collective_id=0, has_side_effects=True, vmem_limit_bytes=VMEM_LIMIT
        ),
        name="whole",
    )(query, key_states, value_states, out_grad, group, doc)
    return tuple(result)


def solution(mesh):
    rows = P(("dp", "seq"), None)
    line = P(("dp", "seq"))
    return jax.shard_map(
        per_device,
        mesh=mesh,
        in_specs=(rows, rows, rows, rows, line, line),
        out_specs=(rows, rows, rows, rows),
        check_vma=False,
    )
```

time: 201 us -> 175 us (0.87)
  Pallas kernels: 193 us -> 166 us
    pallas_call x3 -> x1, Pallas kernels: 193 us -> 166 us  [per_device(): pl.pallas_call(whole_kernel, out_shape=[jax.ShapeDtypeStruct((ROWS, HEADS...]
where the time goes in v2:
time: 175 us; the launch traced here: 172 us
  Pallas kernels  166 us (95%)
  local copies, waits for them, and re-layouts  5.22 us (3%)
    pallas_call x1, Pallas kernels, per_device(): pl.pallas_call(whole_kernel, out_shape=[jax.ShapeDtypeStruct((ROWS, HEADS...  166 us
    unnamed x10, local copies, waits for them, and re-layouts  5.22 us

profile of v2, /device:TPU:32, one launch (start us, length us, event | category | flops | bytes accessed | tf_op | source)
XLA Modules:
  0.0 172.3 jit_solution(3209762055531066984)
XLA Ops:
  0.6 166.4 %whole.1 = (bf16[128,4096]{1,0:T(8,128)(2,1)}, bf16[128,4096]{1,0:T(8,128)(2,1)}, bf16[128,1024]{1,0:T(8,128)(2,1)}, bf16[128,1024]{1,0:T(8,128)(2,1)}) custom-call(bf16[128,4096]{1,0:T(8,128)(2,1)} %q_ref.1, bf16[128,1024]{1,0:T(8,128)(2,1)} %k_ref.1, bf16[128,1024]{1,0:T(8,128)(2,1)} %v_ref.1, bf16[128,4096]{1,0:T(8,128)(2,1)} %g_ref.1, s32[1,128]{1,0:T(1,128)} %bitcast.2, ...), custom_call_target="tpu_custom_call" | custom-call | tf_op jit(solution)/shard_map/whole/pallas_call | solution.py:471
  167.1 0.0 copy-start
  167.1 2.4 %copy.14 = bf16[128,4096]{1,0:T(8,128)(2,1)} copy(bf16[128,4096]{1,0:T(8,128)(2,1)} %get-tuple-element.8) | data formatting | bytes 2097152
  169.5 0.0 copy-done
  169.5 0.0 copy-start.2
  169.5 1.0 copy.15
  170.4 0.1 copy-done.2
  170.6 0.0 copy-start.1
  170.6 0.7 copy.16
  171.3 0.3 copy-done.1
  171.6 0.7 copy.17
Async XLA Ops:
  167.1 2.4 %copy-start = (bf16[128,4096]{1,0:T(8,128)(2,1)S(1)}, bf16[128,4096]{1,0:T(8,128)(2,1)}, u32[]{:S(2)}) copy-start(bf16[128,4096]{1,0:T(8,128)(2,1)} %get-tuple-element.9) | copy-start | bytes 3145732
  169.5 1.1 copy-start.2
  170.6 1.0 copy-start.1

commit v3 on v2

v3 whole, which is shorter than its diff:
```python
import math

import jax
import jax.numpy as jnp
from jax import lax
from jax.experimental import pallas as pl
from jax.experimental.pallas import tpu as pltpu
from jax.sharding import PartitionSpec as P

HD = 128
NX, NZ, NS = 4, 8, 8
NG = NX * NS
CAP = 5
SLOTS = NG * CAP
HALF = SLOTS // 2
KEYS = NZ * SLOTS
HEADS, KVH, RATIO = 32, 8, 4
UNITS = 16
PIECES = 4
ROWS = 128
BLK = 16
SET = KVH // 2
SETS = 2
WIDE = 8
LANES = RATIO * SLOTS
SPLIT = 256
INV_ROOT = 1.0 / math.sqrt(HD)
MESH = pl.DeviceIdType.MESH
BF16 = jnp.bfloat16
F32 = jnp.float32
VMEM_LIMIT = 56 * 1024 * 1024


def iota(shape, dim):
    return lax.broadcasted_iota(jnp.int32, shape, dim)


def dot(a, b):
    return lax.dot_general(a, b, (((1,), (0,)), ((), ())), preferred_element_type=F32)


def dot_nt(a, b):
    return lax.dot_general(a, b, (((1,), (1,)), ((), ())), preferred_element_type=F32)


def place():
    dp, seq = lax.axis_index("dp"), lax.axis_index("seq")
    return dp // NZ, lax.rem(dp, NZ), seq


def plane_device(x, z, seq, step):
    to_x = lax.rem(x + step // NS, NX)
    rest = lax.rem(step, NS)
    to_y = lax.rem(seq // 2 + rest // 2, NS // 2)
    to_core = lax.rem(seq + rest, 2)
    to_seq = to_y * 2 + to_core
    return to_x * NS + to_seq, (to_x * NZ + z, to_seq)


def slot_matrix(group_ref, width):
    across = jnp.broadcast_to(group_ref[...], (ROWS, ROWS)).astype(F32)
    down = across.T
    earlier = (across == down) & (iota((ROWS, ROWS), 0) < iota((ROWS, ROWS), 1))
    rank = jnp.sum(earlier.astype(F32), axis=0, keepdims=True)
    slot = across[:1] * width + rank
    return (iota((NG * width, ROWS), 0).astype(F32) == slot).astype(BF16)


def transposed(matrix):
    return matrix.astype(F32).T.astype(BF16)


def swap_tiles(swap, tiles):
    mixed = dot(swap, jnp.concatenate(tiles, axis=0)).astype(BF16)
    return [mixed[i * 16 : (i + 1) * 16] for i in range(mixed.shape[0] // 16)]


def greet(x, z, seq, ring):
    barrier = pltpu.get_barrier_semaphore()

    def signal(step, carry):
        _, device = plane_device(x, z, seq, step)
        pl.semaphore_signal(barrier, inc=1, device_id=device, device_id_type=MESH)
        return carry

    for device in ring:
        pl.semaphore_signal(barrier, inc=1, device_id=device, device_id_type=MESH)
    lax.fori_loop(1, NG, signal, 0)
    return barrier


def exchange_start(x, z, seq, send, recv, send_sem, recv_sem, own_sem):
    me = x * NS + seq

    def one(step, carry):
        to, device = plane_device(x, z, seq, step)
        pltpu.make_async_remote_copy(
            src_ref=send.at[to],
            dst_ref=recv.at[me],
            send_sem=send_sem,
            recv_sem=recv_sem,
            device_id=device,
            device_id_type=MESH,
        ).start()
        return carry

    lax.fori_loop(1, NG, one, 0)
    pltpu.make_async_copy(send.at[me], recv.at[me], own_sem).start()


def exchange_wait_recv(recv, recv_sem, own_sem):
    pltpu.make_async_copy(recv.at[pl.ds(0, NG - 1)], recv.at[pl.ds(0, NG - 1)], recv_sem).wait()
    pltpu.make_async_copy(recv.at[0], recv.at[0], own_sem).wait()


def exchange_wait_send(send, send_sem):
    pltpu.make_async_copy(send.at[pl.ds(0, NG - 1)], send.at[pl.ds(0, NG - 1)], send_sem).wait()


def token_tiles(ref, piece, block):
    return [ref[piece, t // CAP, t % CAP] for t in range(block * BLK, block * BLK + BLK)]


def put_tiles(ref, piece, block, tiles):
    for i, tile in enumerate(tiles):
        t = block * BLK + i
        ref[piece, t // CAP, t % CAP] = tile


def message_from_wide():
    out, src = iota((192, 256), 0), iota((192, 256), 1)
    group, row, unit = out // 48, lax.rem(out, 48) // 8, lax.rem(out, 8)
    return (src == unit * 32 + group * 8 + row).astype(BF16)


def units_from_message(block):
    out, src = iota((128, 192), 0), iota((128, 192), 1)
    slot = block * BLK + lax.rem(out, BLK) - first_message(block) * CAP
    return (src == (slot // CAP) * 48 + lax.rem(slot, CAP) * 8 + out // BLK).astype(BF16)


def first_message(block):
    return block * BLK // CAP


def message_from_units(four):
    out, src = iota((192, 256), 0), iota((192, 256), 1)
    row, unit = lax.rem(out, 48) // 8, lax.rem(out, 8)
    slot = four * 4 * CAP + (out // 48) * CAP + row - (four * 4 * CAP // BLK) * BLK
    return ((src == unit * 32 + slot) & (row < CAP)).astype(BF16)


def query_slots(rows):
    lane = iota((rows, LANES), 1)
    return (lane // (RATIO * HALF)) * HALF + lax.rem(lane, HALF)


def query_codes(meta):
    expand = (iota((HD, LANES), 0) == lax.rem(query_slots(HD), 20)).astype(BF16)
    own = iota((16, LANES), 0) == 8 + query_slots(16) // 20
    return jnp.sum(jnp.where(own, dot(meta, expand), 0.0), axis=0, keepdims=True)


def mask_block(meta_ref, bias, z, zk):
    tq = query_slots(1)
    code_q = query_codes(meta_ref[z])
    order_q = (tq // 40) * 320 + z * 40 + lax.rem(tq, 40)
    slot, lane = iota((SLOTS, HD), 0), iota((SLOTS, HD), 1)
    spread = (8 + iota((SLOTS, 16), 0) // 20 == iota((SLOTS, 16), 1)).astype(BF16)
    picked = jnp.where(lane == lax.rem(slot, 20), dot(spread, meta_ref[zk]), 0.0).astype(BF16)
    code_k = dot(picked, jnp.ones((HD, HD), BF16))
    order_k = (slot // 40) * 320 + zk * 40 + lax.rem(slot, 40)
    for half in range(2):
        rows = slice(half * HALF, (half + 1) * HALF)
        at_row = pl.multiple_of(half * NZ * HALF + zk * HALF, BLK)
        for at in range(0, LANES, HD):
            cols = slice(at, at + HD)
            ok = (
                (code_k[rows] == code_q[:, cols])
                & (code_k[rows] > 0.5)
                & (order_k[rows] <= order_q[:, cols])
            )
            bias[pl.ds(at_row, HALF), cols] = jnp.where(ok, 0.0, -1e30)


def attend_head(
    c, kv_ref, q_ref, g_ref, o_ref, dq_ref, dkv_ref, bias, p_ref, ds_ref, between
):
    log_scale = INV_ROOT * math.log2(math.e)

    def rows_of(ref):
        return jnp.concatenate(
            [
                ref[c * RATIO + h, half * HALF : (half + 1) * HALF, :]
                for half in range(2)
                for h in range(RATIO)
            ],
            axis=0,
        )

    q, g = rows_of(q_ref), rows_of(g_ref)
    k = kv_ref[c, 0].reshape(KEYS, HD)
    v = kv_ref[c, 1].reshape(KEYS, HD)
    kt, vt, gt = k.T, v.T, g.T
    outs, dqs = [], []
    blocks = ((0, SPLIT, KEYS // 2), (SPLIT, 2 * SPLIT, KEYS), (2 * SPLIT, LANES, KEYS))
    for i, (lo, hi, n) in enumerate(blocks):
        s = dot_nt(k[:n], q[lo:hi]) * log_scale + bias[:n, lo:hi]
        p = jnp.exp2(s - jnp.max(s, axis=0, keepdims=True))
        p = p * (1.0 / jnp.sum(p, axis=0, keepdims=True))
        low = p.astype(BF16)
        p_ref[:n, lo:hi] = low
        between(2 * i)
        out = dot(vt[:, :n], low).astype(BF16)
        delta = jnp.sum(gt[:, lo:hi].astype(F32) * out.astype(F32), axis=0, keepdims=True)
        ds = (p * (dot_nt(v[:n], g[lo:hi]) - delta)).astype(BF16)
        ds_ref[:n, lo:hi] = ds
        outs.append(out.T)
        dqs.append((dot(kt[:, :n], ds) * INV_ROOT).astype(BF16).T)
        between(2 * i + 1)
    out, dq = jnp.concatenate(outs, axis=0), jnp.concatenate(dqs, axis=0)
    for half in range(2):
        for h in range(RATIO):
            rows = slice((half * RATIO + h) * HALF, (half * RATIO + h + 1) * HALF)
            o_ref[c * RATIO + h, half * HALF : (half + 1) * HALF, :] = out[rows]
            dq_ref[c * RATIO + h, half * HALF : (half + 1) * HALF, :] = dq[rows]
    n = KEYS // 2
    for half, lo in ((0, 0), (1, SPLIT)):
        rows = slice(half * n, (half + 1) * n)
        dkv_ref[c, 0, half] = (dot(ds_ref[rows, lo:], q[lo:]) * INV_ROOT).astype(BF16)
        dkv_ref[c, 1, half] = dot(p_ref[rows, lo:], g[lo:]).astype(BF16)
        between(6 + half)


def whole_kernel(
    q_ref, k_ref, v_ref, g_ref, group_ref, doc_ref,
    out_ref, qg_ref, kg_ref, vg_ref,
    kv_ref, meta_ref, qu_ref, gu_ref, ou_ref, dqu_ref, dkv_ref,
    bias, p_ref, ds_ref,
    send0, recv0, send, recv, dkv_send, back0, back, land,
    kv_s, kv_r, kv_o, row_s, row_r, row_o, dkv_s, dkv_r, dkv_o, res_s, res_r, res_o,
    ring_s, ring_r, sum_s, sum_r, meta_s, meta_r,
):
    x, z, seq = place()
    me = x * NS + seq
    right = (x * NZ + lax.rem(z + 1, NZ), seq)
    left = (x * NZ + lax.rem(z + NZ - 1, NZ), seq)
    barrier = greet(x, z, seq, (left, right))

    pick = slot_matrix(group_ref, CAP)
    pick_wide = slot_matrix(group_ref, WIDE)
    row, col = iota((256, 256), 0), iota((256, 256), 1)
    swap = (col == lax.rem(row, 16) * 16 + row // 16).astype(BF16)

    def rows_pack(piece):
        cols = slice(piece * 1024, (piece + 1) * 1024)
        packed = [dot(pick, part[:, cols]).astype(BF16) for part in (q_ref, g_ref)]
        for block in range(SLOTS // BLK):
            rows = slice(block * BLK, (block + 1) * BLK)
            tiles = [part[rows, at * HD : (at + 1) * HD] for part in packed for at in range(8)]
            put_tiles(send, piece, block, swap_tiles(swap, tiles))

    def rows_start(piece):
        exchange_start(
            x, z, seq, send.at[piece], recv.at[piece],
            row_s.at[piece], row_r.at[piece], row_o.at[piece],
        )

    def rows_unpack(piece):
        exchange_wait_recv(recv.at[piece], row_r.at[piece], row_o.at[piece])
        for block in range(SLOTS // BLK):
            tiles = swap_tiles(swap, token_tiles(recv, piece, block))
            rows = slice(block * BLK, (block + 1) * BLK)
            for unit in range(8):
                qu_ref[piece * 8 + unit, rows, :] = tiles[unit]
                gu_ref[piece * 8 + unit, rows, :] = tiles[8 + unit]

    def results_start(piece):
        exchange_wait_send(send.at[piece], row_s.at[piece])
        for block in range(SLOTS // BLK):
            rows = slice(block * BLK, (block + 1) * BLK)
            tiles = [ou_ref[piece * 8 + unit, rows, :] for unit in range(8)]
            tiles += [dqu_ref[piece * 8 + unit, rows, :] for unit in range(8)]
            put_tiles(send, piece, block, swap_tiles(swap, tiles))
        exchange_start(
            x, z, seq, send.at[piece], back.at[piece],
            res_s.at[piece], res_r.at[piece], res_o.at[piece],
        )

    def results_unpack(piece):
        exchange_wait_recv(back.at[piece], res_r.at[piece], res_o.at[piece])
        pick_t = transposed(pick)
        parts = [[] for _ in range(UNITS)]
        for block in range(SLOTS // BLK):
            tiles = swap_tiles(swap, token_tiles(back, piece, block))
            for unit in range(UNITS):
                parts[unit].append(tiles[unit])
        for unit in range(UNITS):
            rows = jnp.concatenate(parts[unit], axis=0)
            at = (piece * 8 + unit % 8) * HD
            (out_ref, qg_ref)[unit // 8][:, at : at + HD] = dot(pick_t, rows).astype(BF16)

    def keys_pack(part, extra, mix):
        packed = []
        for unit in range(8):
            at = (part * SET + unit // 2) * HD
            rows = dot(pick_wide, (k_ref, v_ref)[unit % 2][:, at : at + HD])
            if extra is not None:
                rows = rows + jnp.where(me // 4 == unit, extra, 0.0)
            packed.append(rows.astype(BF16))
        for four in range(NG // 4):
            rows = slice(four * 32, (four + 1) * 32)
            tiles = swap_tiles(mix, [part_rows[rows] for part_rows in packed])
            for i, tile in enumerate(tiles):
                send0[part, four * 4 + i // 3, i % 3] = tile

    def keys_start(part):
        exchange_start(
            x, z, seq, send0.at[part], recv0.at[part],
            kv_s.at[part], kv_r.at[part], kv_o.at[part],
        )

    def keys_unpack(part):
        exchange_wait_recv(recv0.at[part], kv_r.at[part], kv_o.at[part])
        here = pl.multiple_of(z * HALF, BLK)
        for block in range(SLOTS // BLK):
            first = first_message(block)
            tiles = [recv0[part, first + i // 3, i % 3] for i in range(12)]
            tiles = swap_tiles(units_from_message(block), tiles)
            half, at = block // 5, (block % 5) * BLK
            for unit in range(8):
                kv_ref[part * SET + unit // 2, unit % 2, half, pl.ds(here + at, BLK), :] = tiles[
                    unit
                ]

    def terms_start(part):
        for four in range(NG // 4):
            lo = four * 4 * CAP // BLK * BLK
            tiles = []
            for unit in range(8):
                for at in (lo, lo + BLK):
                    half, in_half = at // HALF, at % HALF
                    tiles.append(
                        land[part * SET + unit // 2, unit % 2, NZ - 2, half, in_half : in_half + BLK, :]
                    )
            tiles = swap_tiles(message_from_units(four), tiles)
            for i, tile in enumerate(tiles):
                dkv_send[part, four * 4 + i // 3, i % 3] = tile
        exchange_start(
            x, z, seq, dkv_send.at[part], back0.at[part],
            dkv_s.at[part], dkv_r.at[part], dkv_o.at[part],
        )

    def terms_unpack(part):
        exchange_wait_recv(back0.at[part], dkv_r.at[part], dkv_o.at[part])
        pick_t = transposed(pick_wide)
        mix = transposed(message_from_wide())
        parts = [[] for _ in range(8)]
        for four in range(NG // 4):
            tiles = [back0[part, four * 4 + i // 3, i % 3] for i in range(12)]
            tiles = swap_tiles(mix, tiles)
            for unit in range(8):
                parts[unit] += tiles[2 * unit : 2 * unit + 2]
        for unit in range(8):
            rows = jnp.concatenate(parts[unit], axis=0)
            at = (part * SET + unit // 2) * HD
            (kg_ref, vg_ref)[unit % 2][:, at : at + HD] = dot(pick_t, rows).astype(BF16)

    def plane(index):
        return pl.ds(pl.multiple_of(index * HALF, BLK), HALF)

    def way(head):
        return 1 + lax.rem(head, 2) * (NZ - 2)

    def neighbour(head):
        return (x * NZ + lax.rem(z + way(head), NZ), seq)

    def gather_copy(head, which, step):
        owner = lax.rem(z + (NZ - way(head)) * step, NZ)
        block = kv_ref.at[head, which, :, plane(owner), :]
        return pltpu.make_async_remote_copy(
            src_ref=block,
            dst_ref=block,
            send_sem=ring_s.at[head, which, step],
            recv_sem=ring_r.at[head, which, step],
            device_id=neighbour(head),
            device_id_type=MESH,
        )

    def meta_copy(step):
        owner = lax.rem(z - step + NZ, NZ)
        return pltpu.make_async_remote_copy(
            src_ref=meta_ref.at[owner],
            dst_ref=meta_ref.at[owner],
            send_sem=meta_s.at[step],
            recv_sem=meta_r.at[step],
            device_id=right,
            device_id_type=MESH,
        )

    def terms_for(head, step):
        return plane(lax.rem(z + (NZ - way(head)) * (step + 1), NZ))

    def sum_copy(head, which, step, src):
        return pltpu.make_async_remote_copy(
            src_ref=src,
            dst_ref=land.at[head, which, step],
            send_sem=sum_s.at[head, which, step],
            recv_sem=sum_r.at[head, which, step],
            device_id=neighbour(head),
            device_id_type=MESH,
        )

    def sum_first(head):
        for which in range(2):
            src = dkv_ref.at[head, which, :, terms_for(head, 0), :]
            sum_copy(head, which, 0, src).start()

    def sum_next(head, which, step):
        slot = land.at[head, which, step - 1]
        sum_copy(head, which, step - 1, slot).wait_recv()
        own = dkv_ref[head, which, :, terms_for(head, step), :]
        slot[...] = (own.astype(F32) + slot[...].astype(F32)).astype(BF16)

        def send_on():
            sum_copy(head, which, step, slot).start()

        if isinstance(step, int):
            if step < NZ - 1:
                send_on()
        else:
            pl.when(step < NZ - 1)(send_on)

    code = dot_nt(pick_wide, jnp.broadcast_to(doc_ref[...] + 1, (HD, ROWS)).astype(BF16))
    slot, lane = iota((256, HD), 0), iota((256, HD), 1)
    code = jnp.where(lane == lax.rem(me, 4) * CAP + lax.rem(slot, WIDE), code, 0.0).astype(BF16)
    sel = ((row // WIDE == col // WIDE) & (lax.rem(row, WIDE) == CAP)).astype(BF16)
    mix = message_from_wide()
    keys_pack(0, dot(sel, code), mix)
    pl.semaphore_wait(barrier, NG + 1)
    keys_start(0)
    keys_pack(1, None, mix)
    keys_start(1)
    for piece in range(PIECES):
        rows_pack(piece)

    keys_unpack(0)
    total = recv0[0, 0, 2]
    for s in range(1, NG):
        total = total + recv0[0, s, 2]
    meta_ref[z] = total

    heads = (0, 1, 2, 3)
    for step in range(NZ - 1):
        for which in range(2):
            for head in heads:
                if step > 0:
                    gather_copy(head, which, step - 1).wait_recv()
                gather_copy(head, which, step).start()
        if step > 0:
            meta_copy(step - 1).wait_recv()
        meta_copy(step).start()
        if step < PIECES:
            rows_start(step)
        mask_block(meta_ref, bias, z, lax.rem(z - step + NZ, NZ))
        if step == 4:
            keys_unpack(1)
        if step >= 5:
            rows_unpack(step - 5)
    for which in range(2):
        for head in heads:
            gather_copy(SET + head, which, 0).start()
    meta_copy(NZ - 2).wait_recv()
    mask_block(meta_ref, bias, z, lax.rem(z + 1, NZ))
    for which in range(2):
        for head in heads:
            gather_copy(head, which, NZ - 2).wait_recv()

    refs = (kv_ref, qu_ref, gu_ref, ou_ref, dqu_ref, dkv_ref, bias, p_ref, ds_ref)

    def first_heads(i, carry):
        def between(at):
            step = 2 * i + 1 + at // 4
            which = (at % 4) // 2
            for head in ((0, 1), (2, 3))[at % 2]:

                @pl.when(step < NZ)
                def _():
                    gather_copy(SET + head, which, step - 1).wait_recv()

                @pl.when(step < NZ - 1)
                def _():
                    gather_copy(SET + head, which, step).start()

        attend_head(i, *refs, between)
        sum_first(i)

        @pl.when(lax.rem(i, 2) == 1)
        def _():
            results_start(i // 2)

        @pl.when(i >= 2)
        def _():
            rows_unpack(i)

        return carry

    lax.fori_loop(0, SET, first_heads, 0)

    def other_heads(i, carry):
        def between(at):
            step = 2 * i + 1 + at // 4
            which = (at % 4) // 2
            for head in ((0, 1), (2, 3))[at % 2]:

                @pl.when(step < NZ)
                def _():
                    sum_next(head, which, step)

        attend_head(i + SET, *refs, between)
        sum_first(i + SET)

        @pl.when(lax.rem(i, 2) == 1)
        def _():
            results_start(2 + i // 2)

        return carry

    lax.fori_loop(0, SET, other_heads, 0)
    for step in range(1, NZ):
        for which in range(2):
            for head in heads:
                sum_next(SET + head, which, step)
        if step == 1:
            terms_start(0)
        if step in (3, 4):
            results_unpack(step - 3)
        if step == 6:
            terms_unpack(0)
    terms_start(1)
    for piece in (2, 3):
        results_unpack(piece)
    terms_unpack(1)

    for step in range(NZ - 1):
        for which in range(2):
            for head in range(KVH):
                gather_copy(head, which, step).wait_send()
                sum_copy(head, which, step, land.at[head, which, step]).wait_send()
        meta_copy(step).wait_send()
    for part in range(SETS):
        exchange_wait_send(send0.at[part], kv_s.at[part])
        exchange_wait_send(dkv_send.at[part], dkv_s.at[part])
    for piece in range(PIECES):
        exchange_wait_send(send.at[piece], res_s.at[piece])


def copy_kernel(*refs):
    for src, dst in zip(refs[:4], refs[4:]):
        dst[...] = src[...]


def per_device(query, key_states, value_states, out_grad, target_group, document):
    vmem = pl.BlockSpec(memory_space=pltpu.VMEM)
    blocks = [pl.BlockSpec((ROWS // 4, heads * HD), lambda i: (i, 0)) for heads in (32, 32, 8, 8)]
    dma = pltpu.SemaphoreType.DMA
    group = target_group.reshape(1, ROWS)
    doc = document.reshape(1, ROWS)
    kv_shape = (KVH, 2, 2, NZ * HALF, HD)
    heads_shape = (HEADS, SLOTS, HD)
    piece_shape = (PIECES, NG, CAP, UNITS, HD)
    message_shape = (SETS, NG, 3, 16, HD)
    out_shape = [
        jax.ShapeDtypeStruct((ROWS, HEADS * HD), BF16),
        jax.ShapeDtypeStruct((ROWS, HEADS * HD), BF16),
        jax.ShapeDtypeStruct((ROWS, KVH * HD), BF16),
        jax.ShapeDtypeStruct((ROWS, KVH * HD), BF16),
    ]
    result = pl.pallas_call(
        whole_kernel,
        out_shape=out_shape,
        in_specs=[vmem] * 6,
        out_specs=[vmem] * 4,
        scratch_shapes=[
            pltpu.VMEM(kv_shape, BF16),
            pltpu.VMEM((NZ, 16, HD), BF16),
            pltpu.VMEM(heads_shape, BF16),
            pltpu.VMEM(heads_shape, BF16),
            pltpu.VMEM(heads_shape, BF16),
            pltpu.VMEM(heads_shape, BF16),
            pltpu.VMEM(kv_shape, BF16),
            pltpu.VMEM((KEYS, LANES), F32),
            pltpu.VMEM((KEYS, LANES), BF16),
            pltpu.VMEM((KEYS, LANES), BF16),
            pltpu.VMEM(message_shape, BF16),
            pltpu.VMEM(message_shape, BF16),
            pltpu.VMEM(piece_shape, BF16),
            pltpu.VMEM(piece_shape, BF16),
            pltpu.VMEM(message_shape, BF16),
            pltpu.VMEM(message_shape, BF16),
            pltpu.VMEM(piece_shape, BF16),
            pltpu.VMEM((KVH, 2, NZ - 1, 2, HALF, HD), BF16),
            dma((SETS,)), dma((SETS,)), dma((SETS,)),
            dma((PIECES,)), dma((PIECES,)), dma((PIECES,)),
            dma((SETS,)), dma((SETS,)), dma((SETS,)),
            dma((PIECES,)), dma((PIECES,)), dma((PIECES,)),
            dma((KVH, 2, NZ - 1)), dma((KVH, 2, NZ - 1)),
            dma((KVH, 2, NZ - 1)), dma((KVH, 2, NZ - 1)),
            dma((NZ - 1,)), dma((NZ - 1,)),
        ],
        compiler_params=pltpu.CompilerParams(
            collective_id=0, has_side_effects=True, vmem_limit_bytes=VMEM_LIMIT
        ),
        name="whole",
    )(query, key_states, value_states, out_grad, group, doc)
    return tuple(
        pl.pallas_call(
            copy_kernel,
            out_shape=out_shape,
            grid=(4,),
            in_specs=blocks,
            out_specs=blocks,
            name="place_outputs",
        )(*result)
    )


def solution(mesh):
    rows = P(("dp", "seq"), None)
    line = P(("dp", "seq"))
    return jax.shard_map(
        per_device,
        mesh=mesh,
        in_specs=(rows, rows, rows, rows, line, line),
        out_specs=(rows, rows, rows, rows),
        check_vma=False,
    )
```

time: 175 us -> 160 us (0.914)
  Pallas kernels: 166 us -> 156 us
  local copies, waits for them, and re-layouts: 5.22 us -> 0 us
    pallas_call x1 -> x2, Pallas kernels: 166 us -> 156 us  [the longest x1 152 us: per_device(): pl.pallas_call(whole_kernel, out_shape=out_shape, in_specs=[vmem] * 6, ou...]
    unnamed x10 -> x0, local copies, waits for them, and re-layouts: 5.22 us -> none
where the time goes in v3:
time: 160 us; the launch traced here: 157 us
  Pallas kernels  156 us (98%)
    pallas_call x1, Pallas kernels, per_device(): pl.pallas_call(whole_kernel, out_shape=out_shape, in_specs=[vmem] * 6, ou...  152 us
    pallas_call x1, Pallas kernels, per_device(): pl.pallas_call(copy_kernel, out_shape=out_shape, grid=(4,), in_specs=bloc...  3.86 us

profile of v3, /device:TPU:32, one launch (start us, length us, event | category | flops | bytes accessed | tf_op | source)
XLA Modules:
  0.0 157.1 jit_solution(16549178075058166526)
XLA Ops:
  0.6 152.4 %whole.1 = (bf16[128,4096]{1,0:T(8,128)(2,1)}, bf16[128,4096]{1,0:T(8,128)(2,1)}, bf16[128,1024]{1,0:T(8,128)(2,1)}, bf16[128,1024]{1,0:T(8,128)(2,1)}) custom-call(bf16[128,4096]{1,0:T(8,128)(2,1)} %q_ref.1, bf16[128,1024]{1,0:T(8,128)(2,1)} %k_ref.1, bf16[128,1024]{1,0:T(8,128)(2,1)} %v_ref.1, bf16[128,4096]{1,0:T(8,128)(2,1)} %g_ref.1, s32[1,128]{1,0:T(1,128)} %bitcast.2, ...), custom_call_target="tpu_custom_call" | custom-call | tf_op jit(solution)/shard_map/whole/pallas_call | solution.py:579
  153.0 3.9 %place_outputs.1 = (bf16[128,4096]{1,0:T(8,128)(2,1)}, bf16[128,4096]{1,0:T(8,128)(2,1)}, bf16[128,1024]{1,0:T(8,128)(2,1)}, bf16[128,1024]{1,0:T(8,128)(2,1)}) custom-call(bf16[128,4096]{1,0:T(8,128)(2,1)} %get-tuple-element.8.refs_0_, bf16[128,4096]{1,0:T(8,128)(2,1)} %get-tuple-element.9.refs_1_, bf16[128,1024]{1,0:T(8,128)(2,1)} %get-tuple-element.10.refs_2_, ...), custom_call_target="tpu_custom_call" | custom-call | tf_op jit(solution)/shard_map/place_outputs/pallas_call | solution.py:617

commit v4 on v3

--- a/solution.py
+++ b/solution.py
@@ -49,12 +49,8 @@
 
 
 def plane_device(x, z, seq, step):
-    to_x = lax.rem(x + step // NS, NX)
-    rest = lax.rem(step, NS)
-    to_y = lax.rem(seq // 2 + rest // 2, NS // 2)
-    to_core = lax.rem(seq + rest, 2)
-    to_seq = to_y * 2 + to_core
-    return to_x * NS + to_seq, (to_x * NZ + z, to_seq)
+    to = lax.rem(x * NS + seq + step, NG)
+    return to, (lax.div(to, NS) * NZ + z, lax.rem(to, NS))
 
 
 def slot_matrix(group_ref, width):
@@ -201,35 +197,55 @@
     q, g = rows_of(q_ref), rows_of(g_ref)
     k = kv_ref[c, 0].reshape(KEYS, HD)
     v = kv_ref[c, 1].reshape(KEYS, HD)
-    kt, vt, gt = k.T, v.T, g.T
+    kt, vt = k.T, v.T
+    blocks = ((0, SPLIT, KEYS // 2), (SPLIT, 2 * SPLIT, KEYS), (2 * SPLIT, LANES, KEYS))
     outs, dqs = [], []
-    blocks = ((0, SPLIT, KEYS // 2), (SPLIT, 2 * SPLIT, KEYS), (2 * SPLIT, LANES, KEYS))
-    for i, (lo, hi, n) in enumerate(blocks):
-        s = dot_nt(k[:n], q[lo:hi]) * log_scale + bias[:n, lo:hi]
-        p = jnp.exp2(s - jnp.max(s, axis=0, keepdims=True))
-        p = p * (1.0 / jnp.sum(p, axis=0, keepdims=True))
-        low = p.astype(BF16)
+
+    def products(i):
+        lo, hi, n = blocks[i]
+        return dot_nt(k[:n], q[lo:hi]), dot_nt(v[:n], g[lo:hi])
+
+    def softmax(i, s, dp):
+        lo, hi, n = blocks[i]
+        s = s * log_scale + bias[:n, lo:hi]
+        e = jnp.exp2(s - jnp.max(s, axis=0, keepdims=True))
+        scale = 1.0 / jnp.sum(e, axis=0, keepdims=True)
+        delta = jnp.sum(e * dp, axis=0, keepdims=True) * scale
+        p = e * scale
+        low, ds = p.astype(BF16), (p * (dp - delta)).astype(BF16)
         p_ref[:n, lo:hi] = low
-        between(2 * i)
-        out = dot(vt[:, :n], low).astype(BF16)
-        delta = jnp.sum(gt[:, lo:hi].astype(F32) * out.astype(F32), axis=0, keepdims=True)
-        ds = (p * (dot_nt(v[:n], g[lo:hi]) - delta)).astype(BF16)
         ds_ref[:n, lo:hi] = ds
-        outs.append(out.T)
+        return low, ds
+
+    def results(i, low, ds):
+        n = blocks[i][2]
+        outs.append(dot(vt[:, :n], low).astype(BF16).T)
         dqs.append((dot(kt[:, :n], ds) * INV_ROOT).astype(BF16).T)
-        between(2 * i + 1)
+
+    first, second = products(0), products(1)
+    done = softmax(0, *first)
+    between(0)
+    third = products(2)
+    after = softmax(1, *second)
+    results(0, *done)
+    between(1)
+    done = softmax(2, *third)
+    results(1, *after)
+    between(2)
+    results(2, *done)
+    n = KEYS // 2
+    for half, lo in ((0, 0), (1, SPLIT)):
+        rows = slice(half * n, (half + 1) * n)
+        dkv_ref[c, 0, half] = (dot(ds_ref[rows, lo:], q[lo:]) * INV_ROOT).astype(BF16)
+        dkv_ref[c, 1, half] = dot(p_ref[rows, lo:], g[lo:]).astype(BF16)
+        if half == 0:
+            between(3)
     out, dq = jnp.concatenate(outs, axis=0), jnp.concatenate(dqs, axis=0)
     for half in range(2):
         for h in range(RATIO):
             rows = slice((half * RATIO + h) * HALF, (half * RATIO + h + 1) * HALF)
             o_ref[c * RATIO + h, half * HALF : (half + 1) * HALF, :] = out[rows]
             dq_ref[c * RATIO + h, half * HALF : (half + 1) * HALF, :] = dq[rows]
-    n = KEYS // 2
-    for half, lo in ((0, 0), (1, SPLIT)):
-        rows = slice(half * n, (half + 1) * n)
-        dkv_ref[c, 0, half] = (dot(ds_ref[rows, lo:], q[lo:]) * INV_ROOT).astype(BF16)
-        dkv_ref[c, 1, half] = dot(p_ref[rows, lo:], g[lo:]).astype(BF16)
-        between(6 + half)
 
 
 def whole_kernel(
@@ -440,8 +456,7 @@
     pl.semaphore_wait(barrier, NG + 1)
     keys_start(0)
     keys_pack(1, None, mix)
-    keys_start(1)
-    for piece in range(PIECES):
+    for piece in (0, 1):
         rows_pack(piece)
 
     keys_unpack(0)
@@ -460,7 +475,11 @@
         if step > 0:
             meta_copy(step - 1).wait_recv()
         meta_copy(step).start()
+        if step == 0:
+            keys_start(1)
         if step < PIECES:
+            if step >= 2:
+                rows_pack(step)
             rows_start(step)
         mask_block(meta_ref, bias, z, lax.rem(z - step + NZ, NZ))
         if step == 4:
@@ -478,15 +497,15 @@
 
     refs = (kv_ref, qu_ref, gu_ref, ou_ref, dqu_ref, dkv_ref, bias, p_ref, ds_ref)
 
+    def hop_of(event):
+        pair = lax.rem(event, 2) * 2
+        return 1 + event // 4, lax.rem(event // 2, 2), (pair, pair + 1)
+
     def first_heads(i, carry):
         def between(at):
-            step = 2 * i + 1 + at // 4
-            which = (at % 4) // 2
-            for head in ((0, 1), (2, 3))[at % 2]:
-
-                @pl.when(step < NZ)
-                def _():
-                    gather_copy(SET + head, which, step - 1).wait_recv()
+            step, which, pair = hop_of(7 * i + at)
+            for head in pair:
+                gather_copy(SET + head, which, step - 1).wait_recv()
 
                 @pl.when(step < NZ - 1)
                 def _():
@@ -494,36 +513,39 @@
 
         attend_head(i, *refs, between)
         sum_first(i)
+        between(4)
+
+        @pl.when(i >= 2)
+        def _():
+            rows_unpack(i)
+
+        between(5)
 
         @pl.when(lax.rem(i, 2) == 1)
         def _():
             results_start(i // 2)
 
-        @pl.when(i >= 2)
-        def _():
-            rows_unpack(i)
-
+        between(6)
         return carry
 
     lax.fori_loop(0, SET, first_heads, 0)
 
     def other_heads(i, carry):
         def between(at):
-            step = 2 * i + 1 + at // 4
-            which = (at % 4) // 2
-            for head in ((0, 1), (2, 3))[at % 2]:
-
-                @pl.when(step < NZ)
-                def _():
-                    sum_next(head, which, step)
+            step, which, pair = hop_of(7 * i + at)
+            for head in pair:
+                sum_next(head, which, step)
 
         attend_head(i + SET, *refs, between)
         sum_first(i + SET)
+        between(4)
+        between(5)
 
         @pl.when(lax.rem(i, 2) == 1)
         def _():
             results_start(2 + i // 2)
 
+        between(6)
         return carry
 
     lax.fori_loop(0, SET, other_heads, 0)
@@ -540,29 +562,45 @@
     terms_start(1)
     for piece in (2, 3):
         results_unpack(piece)
-    terms_unpack(1)
-
-    for step in range(NZ - 1):
+
+    def ring_sent(step, carry):
         for which in range(2):
             for head in range(KVH):
                 gather_copy(head, which, step).wait_send()
                 sum_copy(head, which, step, land.at[head, which, step]).wait_send()
         meta_copy(step).wait_send()
+        return carry
+
+    lax.fori_loop(0, NZ - 1, ring_sent, 0)
+    exchange_wait_send(dkv_send.at[0], dkv_s.at[0])
     for part in range(SETS):
         exchange_wait_send(send0.at[part], kv_s.at[part])
-        exchange_wait_send(dkv_send.at[part], dkv_s.at[part])
     for piece in range(PIECES):
         exchange_wait_send(send.at[piece], res_s.at[piece])
+    terms_unpack(1)
+    exchange_wait_send(dkv_send.at[1], dkv_s.at[1])
 
 
 def copy_kernel(*refs):
-    for src, dst in zip(refs[:4], refs[4:]):
-        dst[...] = src[...]
+    srcs, dsts, held, into, out_of = refs[:4], refs[4:8], refs[8:12], refs[12], refs[13]
+    loads, stores = [], []
+    for src, dst, buf in zip(srcs, dsts, held):
+        for part in range(4):
+            rows, n = pl.ds(part * 32, 32), len(loads)
+            loads.append(pltpu.make_async_copy(src.at[rows], buf.at[rows], into.at[n]))
+            stores.append(pltpu.make_async_copy(buf.at[rows], dst.at[rows], out_of.at[n]))
+    for load in loads:
+        load.start()
+    for load, store in zip(loads, stores):
+        load.wait()
+        store.start()
+    for store in stores:
+        store.wait()
 
 
 def per_device(query, key_states, value_states, out_grad, target_group, document):
     vmem = pl.BlockSpec(memory_space=pltpu.VMEM)
-    blocks = [pl.BlockSpec((ROWS // 4, heads * HD), lambda i: (i, 0)) for heads in (32, 32, 8, 8)]
+    anywhere = pl.BlockSpec(memory_space=pl.ANY)
     dma = pltpu.SemaphoreType.DMA
     group = target_group.reshape(1, ROWS)
     doc = document.reshape(1, ROWS)
@@ -617,9 +655,10 @@
         pl.pallas_call(
             copy_kernel,
             out_shape=out_shape,
-            grid=(4,),
-            in_specs=blocks,
-            out_specs=blocks,
+            in_specs=[anywhere] * 4,
+            out_specs=[anywhere] * 4,
+            scratch_shapes=[pltpu.VMEM(shape.shape, BF16) for shape in out_shape]
+            + [dma((16,)), dma((16,))],
             name="place_outputs",
         )(*result)
     )

time: 160 us -> 151 us (0.944); the launches traced: 157 us -> 150 us
  Pallas kernels: 156 us -> 149 us
    pallas_call x1, Pallas kernels: 152 us -> 146 us  [per_device(): pl.pallas_call(whole_kernel, out_shape=out_shape, in_specs=[vmem] * 6, ou...]
where the time goes in v4:
time: 151 us; the launch traced here: 150 us
  Pallas kernels  149 us (99%)
    pallas_call x1, Pallas kernels, per_device(): pl.pallas_call(whole_kernel, out_shape=out_shape, in_specs=[vmem] * 6, ou...  146 us

profile of v4, /device:TPU:32, one launch (start us, length us, event | category | flops | bytes accessed | tf_op | source)
XLA Modules:
  0.0 149.7 jit_solution(15318972995354893123)
XLA Ops:
  0.6 146.2 %whole.1 = (bf16[128,4096]{1,0:T(8,128)(2,1)}, bf16[128,4096]{1,0:T(8,128)(2,1)}, bf16[128,1024]{1,0:T(8,128)(2,1)}, bf16[128,1024]{1,0:T(8,128)(2,1)}) custom-call(bf16[128,4096]{1,0:T(8,128)(2,1)} %q_ref.1, bf16[128,1024]{1,0:T(8,128)(2,1)} %k_ref.1, bf16[128,1024]{1,0:T(8,128)(2,1)} %v_ref.1, bf16[128,4096]{1,0:T(8,128)(2,1)} %g_ref.1, s32[1,128]{1,0:T(1,128)} %bitcast.2, ...), custom_call_target="tpu_custom_call" | custom-call | tf_op jit(solution)/shard_map/whole/pallas_call | solution.py:617
  146.8 2.7 %place_outputs.1 = (bf16[128,4096]{1,0:T(8,128)(2,1)}, bf16[128,4096]{1,0:T(8,128)(2,1)}, bf16[128,1024]{1,0:T(8,128)(2,1)}, bf16[128,1024]{1,0:T(8,128)(2,1)}) custom-call(bf16[128,4096]{1,0:T(8,128)(2,1)} %get-tuple-element.8.refs_0_, bf16[128,4096]{1,0:T(8,128)(2,1)} %get-tuple-element.9.refs_1_, bf16[128,1024]{1,0:T(8,128)(2,1)} %get-tuple-element.10.refs_2_, ...), custom_call_target="tpu_custom_call" | custom-call | tf_op jit(solution)/shard_map/place_outputs/pallas_call | solution.py:655

commit v5 on v4

--- a/solution.py
+++ b/solution.py
@@ -249,8 +249,9 @@
 
 
 def whole_kernel(
-    q_ref, k_ref, v_ref, g_ref, group_ref, doc_ref,
-    out_ref, qg_ref, kg_ref, vg_ref,
+    q_in, k_ref, v_ref, g_in, group_ref, doc_ref,
+    out_hbm, qg_hbm, kg_ref, vg_ref,
+    q_ref, g_ref, out_ref, qg_ref, load_sem, store_sem,
     kv_ref, meta_ref, qu_ref, gu_ref, ou_ref, dqu_ref, dkv_ref,
     bias, p_ref, ds_ref,
     send0, recv0, send, recv, dkv_send, back0, back, land,
@@ -261,7 +262,17 @@
     me = x * NS + seq
     right = (x * NZ + lax.rem(z + 1, NZ), seq)
     left = (x * NZ + lax.rem(z + NZ - 1, NZ), seq)
+    loads = [
+        pltpu.make_async_copy(src, dst, load_sem.at[i])
+        for i, (src, dst) in enumerate(((q_in, q_ref), (g_in, g_ref)))
+    ]
+    stores = [
+        pltpu.make_async_copy(src, dst, store_sem.at[i])
+        for i, (src, dst) in enumerate(((out_ref, out_hbm), (qg_ref, qg_hbm)))
+    ]
     barrier = greet(x, z, seq, (left, right))
+    for load in loads:
+        load.start()
 
     pick = slot_matrix(group_ref, CAP)
     pick_wide = slot_matrix(group_ref, WIDE)
@@ -456,6 +467,8 @@
     pl.semaphore_wait(barrier, NG + 1)
     keys_start(0)
     keys_pack(1, None, mix)
+    for load in loads:
+        load.wait()
     for piece in (0, 1):
         rows_pack(piece)
 
@@ -485,7 +498,7 @@
         if step == 4:
             keys_unpack(1)
         if step >= 5:
-            rows_unpack(step - 5)
+            rows_unpack(step - 5) if step == 5 else None
     for which in range(2):
         for head in heads:
             gather_copy(SET + head, which, 0).start()
@@ -515,7 +528,7 @@
         sum_first(i)
         between(4)
 
-        @pl.when(i >= 2)
+        @pl.when(i >= 1)
         def _():
             rows_unpack(i)
 
@@ -549,19 +562,23 @@
         return carry
 
     lax.fori_loop(0, SET, other_heads, 0)
-    for step in range(1, NZ):
-        for which in range(2):
-            for head in heads:
-                sum_next(SET + head, which, step)
-        if step == 1:
-            terms_start(0)
-        if step in (3, 4):
-            results_unpack(step - 3)
-        if step == 6:
-            terms_unpack(0)
+    beside = {
+        1: lambda: terms_start(0),
+        6: lambda: results_unpack(0),
+        10: lambda: results_unpack(1),
+        18: lambda: terms_unpack(0),
+    }
+    for event in range(4 * (NZ - 1)):
+        step, which, pair = 1 + event // 4, event // 2 % 2, event % 2 * 2
+        for head in (pair, pair + 1):
+            sum_next(SET + head, which, step)
+        if event in beside:
+            beside[event]()
     terms_start(1)
     for piece in (2, 3):
         results_unpack(piece)
+    for store in stores:
+        store.start()
 
     def ring_sent(step, carry):
         for which in range(2):
@@ -579,6 +596,8 @@
         exchange_wait_send(send.at[piece], res_s.at[piece])
     terms_unpack(1)
     exchange_wait_send(dkv_send.at[1], dkv_s.at[1])
+    for store in stores:
+        store.wait()
 
 
 def copy_kernel(*refs):
@@ -617,9 +636,14 @@
     result = pl.pallas_call(
         whole_kernel,
         out_shape=out_shape,
-        in_specs=[vmem] * 6,
-        out_specs=[vmem] * 4,
+        in_specs=[anywhere, vmem, vmem, anywhere, vmem, vmem],
+        out_specs=[anywhere, anywhere, vmem, vmem],
         scratch_shapes=[
+            pltpu.VMEM((ROWS, HEADS * HD), BF16),
+            pltpu.VMEM((ROWS, HEADS * HD), BF16),
+            pltpu.VMEM((ROWS, HEADS * HD), BF16),
+            pltpu.VMEM((ROWS, HEADS * HD), BF16),
+            dma((2,)), dma((2,)),
             pltpu.VMEM(kv_shape, BF16),
             pltpu.VMEM((NZ, 16, HD), BF16),
             pltpu.VMEM(heads_shape, BF16),

time: 151 us -> 150 us (level)
  no operation moved by 1% of the time
where the time goes in v5:
time: 150 us; the launch traced here: 148 us
  Pallas kernels  148 us (99%)
    pallas_call x1, Pallas kernels, per_device(): pl.pallas_call(whole_kernel, out_shape=out_shape, in_specs=[anywhere, vme...  145 us

profile of v5, /device:TPU:32, one launch (start us, length us, event | category | flops | bytes accessed | tf_op | source)
XLA Modules:
  0.0 148.4 jit_solution(17526228528668459020)
XLA Ops:
  0.6 144.9 %whole.1 = (bf16[128,4096]{1,0:T(8,128)(2,1)}, bf16[128,4096]{1,0:T(8,128)(2,1)}, bf16[128,1024]{1,0:T(8,128)(2,1)}, bf16[128,1024]{1,0:T(8,128)(2,1)}) custom-call(bf16[128,4096]{1,0:T(8,128)(2,1)} %q_in.1, bf16[128,1024]{1,0:T(8,128)(2,1)} %k_ref.1, bf16[128,1024]{1,0:T(8,128)(2,1)} %v_ref.1, bf16[128,4096]{1,0:T(8,128)(2,1)} %g_in.1, s32[1,128]{1,0:T(1,128)} %bitcast.2, ...), custom_call_target="tpu_custom_call" | custom-call | tf_op jit(solution)/shard_map/whole/pallas_call | solution.py:636
  145.5 2.7 %place_outputs.1 = (bf16[128,4096]{1,0:T(8,128)(2,1)}, bf16[128,4096]{1,0:T(8,128)(2,1)}, bf16[128,1024]{1,0:T(8,128)(2,1)}, bf16[128,1024]{1,0:T(8,128)(2,1)}) custom-call(bf16[128,4096]{1,0:T(8,128)(2,1)} %get-tuple-element.8.refs_0_, bf16[128,4096]{1,0:T(8,128)(2,1)} %get-tuple-element.9.refs_1_, bf16[128,1024]{1,0:T(8,128)(2,1)} %get-tuple-element.10.refs_2_, ...), custom_call_target="tpu_custom_call" | custom-call | tf_op jit(solution)/shard_map/place_outputs/pallas_call | solution.py:679

commit v6 on v5

--- a/solution.py
+++ b/solution.py
@@ -49,7 +49,7 @@
 
 
 def plane_device(x, z, seq, step):
-    to = lax.rem(x * NS + seq + step, NG)
+    to = lax.rem(x * NS + seq + step * 11, NG)
     return to, (lax.div(to, NS) * NZ + z, lax.rem(to, NS))
 
 

time: 150 us -> 150 us (level)
  no operation moved by 1% of the time
where the time goes in v6:
time: 150 us; the launch traced here: 149 us
  Pallas kernels  148 us (99%)
    pallas_call x1, Pallas kernels, per_device(): pl.pallas_call(whole_kernel, out_shape=out_shape, in_specs=[anywhere, vme...  145 us

profile of v6, /device:TPU:32, one launch (start us, length us, event | category | flops | bytes accessed | tf_op | source)
XLA Modules:
  0.0 148.8 jit_solution(15338320607074390607)
XLA Ops:
  0.6 145.3 %whole.1 = (bf16[128,4096]{1,0:T(8,128)(2,1)}, bf16[128,4096]{1,0:T(8,128)(2,1)}, bf16[128,1024]{1,0:T(8,128)(2,1)}, bf16[128,1024]{1,0:T(8,128)(2,1)}) custom-call(bf16[128,4096]{1,0:T(8,128)(2,1)} %q_in.1, bf16[128,1024]{1,0:T(8,128)(2,1)} %k_ref.1, bf16[128,1024]{1,0:T(8,128)(2,1)} %v_ref.1, bf16[128,4096]{1,0:T(8,128)(2,1)} %g_in.1, s32[1,128]{1,0:T(1,128)} %bitcast.2, ...), custom_call_target="tpu_custom_call" | custom-call | tf_op jit(solution)/shard_map/whole/pallas_call | solution.py:636
  145.9 2.7 %place_outputs.1 = (bf16[128,4096]{1,0:T(8,128)(2,1)}, bf16[128,4096]{1,0:T(8,128)(2,1)}, bf16[128,1024]{1,0:T(8,128)(2,1)}, bf16[128,1024]{1,0:T(8,128)(2,1)}) custom-call(bf16[128,4096]{1,0:T(8,128)(2,1)} %get-tuple-element.8.refs_0_, bf16[128,4096]{1,0:T(8,128)(2,1)} %get-tuple-element.9.refs_1_, bf16[128,1024]{1,0:T(8,128)(2,1)} %get-tuple-element.10.refs_2_, ...), custom_call_target="tpu_custom_call" | custom-call | tf_op jit(solution)/shard_map/place_outputs/pallas_call | solution.py:679
